TPU v7x, 32 devices: a whole 2x2x4 slice. The times are simulated.
32 devices in a mesh: rows: 16 (over z, y, x), rep: 2 (over core).
Axes of the slice: x: 2, y: 2, z: 4, core: 2. Of those that a mesh axis runs over, the one named last changes fastest.
Arguments:
- margin_blocks: float32 [64, 16, 128, 128], P('rows', 'rep'), may hold values from -1 to 1
- margin_cols: int32 [64, 16], P('rows', 'rep'), may hold values from 0 to 63, as said below
- factor_blocks: float32 [64, 16, 128, 128], P('rows'), may hold values from -0.5 to 0.5
- factor_cols: int32 [64, 16], P('rows'), may hold values from 0 to 63, as said below
- product_cols: int32 [64, 24], P('rows'), may hold values from 0 to 63, as said below
- metric_cols: int32 [64, 24], P('rows'), may hold values from 0 to 63, as said below
Outputs:
- product: float32 [64, 24, 128, 128], P('rows', 'rep')
- metric: float32 [64, 24, 128, 128], P('rows', 'rep')
Inputs may be any that keep to these rules, and one draw needn't show every extreme that they name: `margin_cols`: each block row holds 16 distinct block columns, its own index among them, each within 8 of the row index cyclically modulo 64. `factor_cols`: each block row holds 16 distinct block columns, each in the block rows of an index of rows at most 2 away from the row's own (column // 4 against row // 4, cyclically); every block column is named by exactly 16 block rows. `product_cols`: each block row holds 24 distinct block columns, its own index among them, each within 16 of the row index cyclically. `metric_cols`: each block row holds 24 distinct block columns, its own index among them, each within 16 of the row index cyclically.
All inputs are finite; a program needn't handle non-finite values.
Results may differ from a plain program's by a relative error of at most 0.0003.
Values sent between devices are 32-bit elements; how exact they have to be, the bound alone decides.
A program may use at most 192 MiB of HBM per device.

v0:
```python
import jax
import jax.numpy as jnp
from jax import lax
from jax.sharding import PartitionSpec as P

HIGHEST = lax.Precision.HIGHEST
OFFSETS = (-2, -1, 1, 2)


def passed_along(array, axis, by):
    devices = lax.axis_size(axis)
    return lax.ppermute(array, axis, [(i, (i + by) % devices) for i in range(devices)])


def shards(margin_blocks, margin_cols, factor_blocks, factor_cols, product_cols, metric_cols):
    row_count = factor_blocks.shape[0]
    slots_factor = factor_blocks.shape[1]
    block_size = factor_blocks.shape[2]
    cycle_size = lax.axis_size("rows")
    position = lax.axis_index("rows")
    core_index = lax.axis_index("rep")
    total_rows = row_count * cycle_size
    first_row = (position - 2) * row_count
    patterns = jnp.concatenate([factor_cols, product_cols], axis=1)
    pattern_layers = {}
    for offset in OFFSETS:
        pattern_layers[offset] = passed_along(patterns, "rows", -offset)
    halo_patterns = jnp.concatenate(
        [pattern_layers[-2], pattern_layers[-1], patterns, pattern_layers[1], pattern_layers[2]],
        axis=0,
    )
    halo_factor_cols = halo_patterns[:, :slots_factor]
    halo_product_cols = halo_patterns[:, slots_factor:]
    factor_layers = {}
    for offset in OFFSETS:
        factor_layers[offset] = passed_along(factor_blocks, "rows", -offset)
    halo_factor = jnp.concatenate(
        [factor_layers[-2], factor_layers[-1], factor_blocks, factor_layers[1], factor_layers[2]],
        axis=0,
    )
    relative = (margin_cols - first_row) % total_rows

    def product_row(packed):
        margin_row, relative_row, kept_row = packed
        picked = halo_factor[relative_row]
        partial_terms = jnp.einsum("kab,kmbc->kmac", margin_row, picked, precision=HIGHEST)
        selector = (halo_factor_cols[relative_row][:, :, None] == kept_row[None, None, :]).astype(
            jnp.float32
        )
        return jnp.einsum("kmy,kmac->yac", selector, partial_terms, precision=HIGHEST)

    partial_product = lax.map(product_row, (margin_blocks, relative, product_cols))
    product = lax.psum_scatter(partial_product, "rep", scatter_dimension=1, tiled=True)
    product_width = product.shape[1]
    product_layers = {}
    for offset in OFFSETS:
        product_layers[offset] = passed_along(product, "rows", -offset)
    halo_product = jnp.concatenate(
        [product_layers[-2], product_layers[-1], product, product_layers[1], product_layers[2]],
        axis=0,
    )
    halo_product_share = lax.dynamic_slice_in_dim(
        halo_product_cols, core_index * product_width, product_width, 1
    )
    flat_cols = halo_factor_cols.reshape(-1)
    entry_count = flat_cols.shape[0]
    targets = position * row_count + jnp.arange(row_count, dtype=jnp.int32)
    matches = (flat_cols[None, :] == targets[:, None]).astype(jnp.int32)
    ranking = jnp.cumsum(matches, axis=1) - 1
    slot_range = jnp.arange(slots_factor, dtype=jnp.int32)
    chosen = matches[:, None, :] * (ranking[:, None, :] == slot_range[None, :, None]).astype(
        jnp.int32
    )
    entries = jnp.sum(chosen * jnp.arange(entry_count, dtype=jnp.int32)[None, None, :], axis=2)
    flat_factor = halo_factor.reshape(-1, block_size, block_size)

    def metric_row(packed):
        entry_row, kept_row = packed
        source_rows = entry_row // slots_factor
        factor_here = flat_factor[entry_row]
        product_here = halo_product[source_rows]
        partial_terms = jnp.einsum("tba,tybc->tyac", factor_here, product_here, precision=HIGHEST)
        selector = (halo_product_share[source_rows][:, :, None] == kept_row[None, None, :]).astype(
            jnp.float32
        )
        return jnp.einsum("tyx,tyac->xac", selector, partial_terms, precision=HIGHEST)

    partial_metric = lax.map(metric_row, (entries, metric_cols))
    metric = lax.psum_scatter(partial_metric, "rep", scatter_dimension=1, tiled=True)
    return (product, metric)


def solution(mesh):
    return jax.shard_map(
        shards,
        mesh=mesh,
        in_specs=(
            P("rows", "rep", None, None),
            P("rows", "rep"),
            P("rows", None, None, None),
            P("rows", None),
            P("rows", None),
            P("rows", None),
        ),
        out_specs=(P("rows", "rep", None, None), P("rows", "rep", None, None)),
        check_vma=False,
    )
```

profile of v0, /device:TPU:1, one launch (start us, length us, event | category | flops | bytes accessed | tf_op | source)
XLA Modules:
  0.0 1067.1 jit_solution(6263807698444152722)
XLA Ops:
  10.5 3.9 collective-permute-start.6
  16.6 262.0 %collective-permute-done = s32[4,40]{1,0:T(4,128)S(1)} collective-permute-done((s32[4,40]{1,0:T(4,128)S(1)}, s32[4,40]{1,0:T(4,128)S(1)}, u32[]{:S(2)}, u32[]{:S(2)}) %collective-permute-start) | collective-permute-done | bytes 672 | tf_op jit(solution)/shard_map/ppermute | solution.py:12
  279.9 6.0 collective-permute-done.1
  305.2 5.0 copy-done.1
  310.2 185.1 %while.22 = (s32[]{:T(128)}, f32[4,24,128,128]{3,2,1,0:T(8,128)}, s32[4,8]{1,0:T(4,128)S(1)}, s32[20,16]{1,0:T(8,128)S(1)}, s32[4,24]{1,0:T(4,128)}, /*index=5*/...) while((s32[]{:T(128)}, f32[4,24,128,128]{3,2,1,0:T(8,128)}, s32[4,8]{1,0:T(4,128)S(1)}, ...), condition=%wide.region_1.2_spmd, body=%wide.region_0.1_spmd.sunk | while | flops 3825209344 | bytes 63970332 | solution.py:52
  310.2 11.4 %gather_fusion = f32[8,16,128,128]{3,2,1,0:T(8,128)} fusion(f32[20,16,128,128]{3,2,1,0:T(8,128)} %get-tuple-element.278, s32[1024]{0:T(1024)S(1)} %pad_clamp_fusion.5), kind=kCustom, calls=%fused_computation.1.clone.1 | custom fusion | bytes 16777248 | tf_op jit(solution)/shard_map/while/body/eval_jaxpr/gather | solution.py:45
  321.6 17.5 %convolution_bitcast_fusion.8 = f32[8,16,128,128]{2,3,1,0:T(8,128)} fusion(f32[8,16,128,128]{3,2,1,0:T(8,128)} %gather_fusion, f32[4,8,128,128]{3,2,1,0:T(8,128)} %get-tuple-element.279, s32[]{:T(128)} %get-tuple-element.265), kind=kOutput, calls=%fused_computation.5.clone.1 | convolution fusion | flops 3221225472 | bytes 17302016 | tf_op jit(solution)/shard_map/while/body/eval_jaxpr/kab,kmbc->kmac/dot_general | solution.py:46
  339.1 9.3 copy.56
  349.7 5.3 convolution_bitcast_fusion.9
  356.4 11.4 %gather_fusion = f32[8,16,128,128]{3,2,1,0:T(8,128)} fusion(f32[20,16,128,128]{3,2,1,0:T(8,128)} %get-tuple-element.278, s32[1024]{0:T(1024)S(1)} %pad_clamp_fusion.5), kind=kCustom, calls=%fused_computation.1.clone.1 | custom fusion | bytes 16777248 | tf_op jit(solution)/shard_map/while/body/eval_jaxpr/gather | solution.py:45
  367.8 17.5 %convolution_bitcast_fusion.8 = f32[8,16,128,128]{2,3,1,0:T(8,128)} fusion(f32[8,16,128,128]{3,2,1,0:T(8,128)} %gather_fusion, f32[4,8,128,128]{3,2,1,0:T(8,128)} %get-tuple-element.279, s32[]{:T(128)} %get-tuple-element.265), kind=kOutput, calls=%fused_computation.5.clone.1 | convolution fusion | flops 3221225472 | bytes 17302016 | tf_op jit(solution)/shard_map/while/body/eval_jaxpr/kab,kmbc->kmac/dot_general | solution.py:46
  385.4 9.3 copy.56
  395.9 5.3 convolution_bitcast_fusion.9
  402.7 11.4 %gather_fusion = f32[8,16,128,128]{3,2,1,0:T(8,128)} fusion(f32[20,16,128,128]{3,2,1,0:T(8,128)} %get-tuple-element.278, s32[1024]{0:T(1024)S(1)} %pad_clamp_fusion.5), kind=kCustom, calls=%fused_computation.1.clone.1 | custom fusion | bytes 16777248 | tf_op jit(solution)/shard_map/while/body/eval_jaxpr/gather | solution.py:45
  414.1 17.5 %convolution_bitcast_fusion.8 = f32[8,16,128,128]{2,3,1,0:T(8,128)} fusion(f32[8,16,128,128]{3,2,1,0:T(8,128)} %gather_fusion, f32[4,8,128,128]{3,2,1,0:T(8,128)} %get-tuple-element.279, s32[]{:T(128)} %get-tuple-element.265), kind=kOutput, calls=%fused_computation.5.clone.1 | convolution fusion | flops 3221225472 | bytes 17302016 | tf_op jit(solution)/shard_map/while/body/eval_jaxpr/kab,kmbc->kmac/dot_general | solution.py:46
  431.6 9.3 copy.56
  442.2 5.3 convolution_bitcast_fusion.9
  449.0 11.4 %gather_fusion = f32[8,16,128,128]{3,2,1,0:T(8,128)} fusion(f32[20,16,128,128]{3,2,1,0:T(8,128)} %get-tuple-element.278, s32[1024]{0:T(1024)S(1)} %pad_clamp_fusion.5), kind=kCustom, calls=%fused_computation.1.clone.1 | custom fusion | bytes 16777248 | tf_op jit(solution)/shard_map/while/body/eval_jaxpr/gather | solution.py:45
  460.4 17.5 %convolution_bitcast_fusion.8 = f32[8,16,128,128]{2,3,1,0:T(8,128)} fusion(f32[8,16,128,128]{3,2,1,0:T(8,128)} %gather_fusion, f32[4,8,128,128]{3,2,1,0:T(8,128)} %get-tuple-element.279, s32[]{:T(128)} %get-tuple-element.265), kind=kOutput, calls=%fused_computation.5.clone.1 | convolution fusion | flops 3221225472 | bytes 17302016 | tf_op jit(solution)/shard_map/while/body/eval_jaxpr/kab,kmbc->kmac/dot_general | solution.py:46
  477.9 9.3 copy.56
  488.5 5.3 convolution_bitcast_fusion.9
  496.8 39.2 %all-reduce.6.cloned.1.call-done = f32[4,24,128,128]{3,2,1,0:T(8,128)} async-done(((f32[4,24,128,128]{3,2,1,0:T(8,128)}), f32[4,24,128,128]{3,2,1,0:T(8,128)}) %all-reduce.6.cloned.1.call-update) | async-done | bytes 6291472
  536.0 3.9 constant_dynamic-slice_fusion.5
  542.6 3.9 collective-permute-start.10
  548.7 195.1 %collective-permute-done.8 = f32[4,12,128,128]{3,2,1,0:T(8,128)} collective-permute-done((f32[4,12,128,128]{3,2,1,0:T(8,128)}, f32[4,12,128,128]{3,2,1,0:T(8,128)}, u32[]{:S(2)}, u32[]{:S(2)}) %collective-permute-start.8) | collective-permute-done | bytes 3145760 | tf_op jit(solution)/shard_map/ppermute | solution.py:12
  760.0 261.5 %while.23 = (s32[]{:T(128)}, f32[4,24,128,128]{3,2,1,0:T(8,128)}, s32[4,16]{1,0:T(4,128)S(1)}, s32[20,12]{1,0:T(8,128)S(1)}, s32[4,24]{1,0:T(4,128)}, /*index=5*...) while((s32[]{:T(128)}, f32[4,24,128,128]{3,2,1,0:T(8,128)}, s32[4,16]{1,0:T(4,128)S(1)}, ...), condition=%wide.region_7.8_spmd, body=%wide.region_6.7_spmd.sunk | while | flops 5737815040 | bytes 95958136 | solution.py:88
  760.1 11.3 %gather_fusion.2 = f32[16,12,128,128]{3,2,1,0:T(8,128)} fusion(f32[20,12,128,128]{3,2,1,0:T(8,128)} %get-tuple-element.302, s32[1024]{0:T(1024)S(1)} %get-tuple-element.255), kind=kCustom, calls=%fused_computation.3.clone.1 | custom fusion | bytes 25165888 | tf_op jit(solution)/shard_map/while/body/eval_jaxpr/gather | solution.py:81
  771.4 7.6 gather_fusion.3
  779.0 23.8 %convolution_bitcast_fusion.10 = f32[16,12,128,128]{2,3,1,0:T(8,128)} fusion(f32[16,12,128,128]{3,2,1,0:T(8,128)} %gather_fusion.2, f32[16,128,128]{2,1,0:T(8,128)S(1)} %gather_fusion.3), kind=kOutput, calls=%fused_computation.22.clone.1 | convolution fusion | flops 4831838208 | bytes 26214400 | tf_op jit(solution)/shard_map/while/body/eval_jaxpr/tba,tybc->tyac/dot_general | solution.py:82
  802.8 12.7 %copy.58 = f32[16,12,128,128]{3,0,1,2:T(8,128)} copy(f32[16,12,128,128]{2,3,1,0:T(8,128)} %convolution_bitcast_fusion.10) | data formatting | bytes 25165824 | tf_op jit(solution)/shard_map/while/body/eval_jaxpr/tba,tybc->tyac/transpose | solution.py:82
  816.9 7.1 convolution_bitcast_fusion.11
  825.4 11.3 %gather_fusion.2 = f32[16,12,128,128]{3,2,1,0:T(8,128)} fusion(f32[20,12,128,128]{3,2,1,0:T(8,128)} %get-tuple-element.302, s32[1024]{0:T(1024)S(1)} %get-tuple-element.255), kind=kCustom, calls=%fused_computation.3.clone.1 | custom fusion | bytes 25165888 | tf_op jit(solution)/shard_map/while/body/eval_jaxpr/gather | solution.py:81
  836.8 7.6 gather_fusion.3
  844.4 23.8 %convolution_bitcast_fusion.10 = f32[16,12,128,128]{2,3,1,0:T(8,128)} fusion(f32[16,12,128,128]{3,2,1,0:T(8,128)} %gather_fusion.2, f32[16,128,128]{2,1,0:T(8,128)S(1)} %gather_fusion.3), kind=kOutput, calls=%fused_computation.22.clone.1 | convolution fusion | flops 4831838208 | bytes 26214400 | tf_op jit(solution)/shard_map/while/body/eval_jaxpr/tba,tybc->tyac/dot_general | solution.py:82
  868.1 12.7 %copy.58 = f32[16,12,128,128]{3,0,1,2:T(8,128)} copy(f32[16,12,128,128]{2,3,1,0:T(8,128)} %convolution_bitcast_fusion.10) | data formatting | bytes 25165824 | tf_op jit(solution)/shard_map/while/body/eval_jaxpr/tba,tybc->tyac/transpose | solution.py:82
  882.2 7.1 convolution_bitcast_fusion.11
  890.8 11.3 %gather_fusion.2 = f32[16,12,128,128]{3,2,1,0:T(8,128)} fusion(f32[20,12,128,128]{3,2,1,0:T(8,128)} %get-tuple-element.302, s32[1024]{0:T(1024)S(1)} %get-tuple-element.255), kind=kCustom, calls=%fused_computation.3.clone.1 | custom fusion | bytes 25165888 | tf_op jit(solution)/shard_map/while/body/eval_jaxpr/gather | solution.py:81
  902.2 7.6 gather_fusion.3
  909.7 23.8 %convolution_bitcast_fusion.10 = f32[16,12,128,128]{2,3,1,0:T(8,128)} fusion(f32[16,12,128,128]{3,2,1,0:T(8,128)} %gather_fusion.2, f32[16,128,128]{2,1,0:T(8,128)S(1)} %gather_fusion.3), kind=kOutput, calls=%fused_computation.22.clone.1 | convolution fusion | flops 4831838208 | bytes 26214400 | tf_op jit(solution)/shard_map/while/body/eval_jaxpr/tba,tybc->tyac/dot_general | solution.py:82
  933.5 12.7 %copy.58 = f32[16,12,128,128]{3,0,1,2:T(8,128)} copy(f32[16,12,128,128]{2,3,1,0:T(8,128)} %convolution_bitcast_fusion.10) | data formatting | bytes 25165824 | tf_op jit(solution)/shard_map/while/body/eval_jaxpr/tba,tybc->tyac/transpose | solution.py:82
  947.6 7.1 convolution_bitcast_fusion.11
  956.2 11.3 %gather_fusion.2 = f32[16,12,128,128]{3,2,1,0:T(8,128)} fusion(f32[20,12,128,128]{3,2,1,0:T(8,128)} %get-tuple-element.302, s32[1024]{0:T(1024)S(1)} %get-tuple-element.255), kind=kCustom, calls=%fused_computation.3.clone.1 | custom fusion | bytes 25165888 | tf_op jit(solution)/shard_map/while/body/eval_jaxpr/gather | solution.py:81
  967.5 7.6 gather_fusion.3
  975.1 23.8 %convolution_bitcast_fusion.10 = f32[16,12,128,128]{2,3,1,0:T(8,128)} fusion(f32[16,12,128,128]{3,2,1,0:T(8,128)} %gather_fusion.2, f32[16,128,128]{2,1,0:T(8,128)S(1)} %gather_fusion.3), kind=kOutput, calls=%fused_computation.22.clone.1 | convolution fusion | flops 4831838208 | bytes 26214400 | tf_op jit(solution)/shard_map/while/body/eval_jaxpr/tba,tybc->tyac/dot_general | solution.py:82
  998.9 12.7 %copy.58 = f32[16,12,128,128]{3,0,1,2:T(8,128)} copy(f32[16,12,128,128]{2,3,1,0:T(8,128)} %convolution_bitcast_fusion.10) | data formatting | bytes 25165824 | tf_op jit(solution)/shard_map/while/body/eval_jaxpr/tba,tybc->tyac/transpose | solution.py:82
  1013.0 7.1 convolution_bitcast_fusion.11
  1021.5 34.8 %all-reduce.8.cloned.1.call-done = f32[4,24,128,128]{3,2,1,0:T(8,128)} async-done(((f32[4,24,128,128]{3,2,1,0:T(8,128)}), f32[4,24,128,128]{3,2,1,0:T(8,128)}) %all-reduce.8.cloned.1.call-update) | async-done | bytes 6291472
  1056.4 3.9 constant_dynamic-slice_fusion.4
  (109 shorter events, 70.2 us)
Async XLA Ops:
  7.2 528.8 %all-reduce.6.cloned.1.call-start = ((), (), s32[]{:S(2)}) async-start(), calls=%async_computation | async-start | bytes 12582912
  7.2 283.6 %collective-permute-start.4 = (f32[4,16,128,128]{3,2,1,0:T(8,128)}, f32[4,16,128,128]{3,2,1,0:T(8,128)}, u32[]{:S(2)}, u32[]{:S(2)}) collective-permute-start(f32[4,16,128,128]{3,2,1,0:T(8,128)} %param.12), channel_id=1, source_target_pairs={{0,4},{2,6},{4,8},{6,10},{8,12},{10,14},{12,16},{14,18},{16,20},{1... | collective-permute-start | bytes 12582920 | tf_op jit(solution)/shard_map/ppermute | solution.py:12
  9.3 284.1 %collective-permute-start.5 = (f32[4,16,128,128]{3,2,1,0:T(8,128)}, f32[4,16,128,128]{3,2,1,0:T(8,128)}, u32[]{:S(2)}, u32[]{:S(2)}) collective-permute-start(f32[4,16,128,128]{3,2,1,0:T(8,128)} %param.12), channel_id=1, source_target_pairs={{0,2},{2,4},{4,6},{6,8},{8,10},{10,12},{12,14},{14,16},{16,18},{18... | collective-permute-start | bytes 12582920 | tf_op jit(solution)/shard_map/ppermute | solution.py:12
  10.5 285.8 %collective-permute-start.6 = (f32[4,16,128,128]{3,2,1,0:T(8,128)}, f32[4,16,128,128]{3,2,1,0:T(8,128)}, u32[]{:S(2)}, u32[]{:S(2)}) collective-permute-start(f32[4,16,128,128]{3,2,1,0:T(8,128)} %param.12), channel_id=1, source_target_pairs={{0,30},{2,0},{4,2},{6,4},{8,6},{10,8},{12,10},{14,12},{16,14},{18,... | collective-permute-start | bytes 12582920 | tf_op jit(solution)/shard_map/ppermute | solution.py:12
  14.4 284.5 %collective-permute-start.7 = (f32[4,16,128,128]{3,2,1,0:T(8,128)}, f32[4,16,128,128]{3,2,1,0:T(8,128)}, u32[]{:S(2)}, u32[]{:S(2)}) collective-permute-start(f32[4,16,128,128]{3,2,1,0:T(8,128)} %param.12), channel_id=1, source_target_pairs={{0,28},{2,30},{4,0},{6,2},{8,4},{10,6},{12,8},{14,10},{16,12},{18,... | collective-permute-start | bytes 12582920 | tf_op jit(solution)/shard_map/ppermute | solution.py:12
  15.6 263.1 %collective-permute-start = (s32[4,40]{1,0:T(4,128)S(1)}, s32[4,40]{1,0:T(4,128)S(1)}, u32[]{:S(2)}, u32[]{:S(2)}) collective-permute-start(s32[4,40]{1,0:T(4,128)S(1)} %pad_add_fusion), channel_id=1, source_target_pairs={{0,4},{2,6},{4,8},{6,10},{8,12},{10,14},{12,16},{14,18},{16,20},{1... | collective-permute-start | bytes 1928 | tf_op jit(solution)/shard_map/ppermute | solution.py:12
  278.7 7.2 collective-permute-start.1
  285.8 2.4 collective-permute-start.2
  288.3 2.4 collective-permute-start.3
  290.8 5.1 copy-start.2
  301.3 8.8 copy-start.1
  310.2 185.4 %copy-start.3 = (u32[32]{0:T(128)S(1)}, u32[32]{0:T(128)}, u32[]{:S(2)}) copy-start(u32[32]{0:T(128)} %constant.122) | copy-start | bytes 388
  495.3 561.1 %all-reduce.8.cloned.1.call-start = ((), (), s32[]{:S(2)}) async-start(), calls=%async_computation.1 | async-start | bytes 12582912
  539.9 204.0 %collective-permute-start.8 = (f32[4,12,128,128]{3,2,1,0:T(8,128)}, f32[4,12,128,128]{3,2,1,0:T(8,128)}, u32[]{:S(2)}, u32[]{:S(2)}) collective-permute-start(f32[4,12,128,128]{3,2,1,0:T(8,128)} %constant_dynamic-slice_fusion.5), channel_id=1, source_target_pairs={{0,4},{2,6},{4,8},{6,10},{8,12},{10,14},{12,16},{14,18},{16,20},{1... | collective-permute-start | bytes 9437192 | tf_op jit(solution)/shard_map/ppermute | solution.py:12
  541.4 204.5 %collective-permute-start.9 = (f32[4,12,128,128]{3,2,1,0:T(8,128)}, f32[4,12,128,128]{3,2,1,0:T(8,128)}, u32[]{:S(2)}, u32[]{:S(2)}) collective-permute-start(f32[4,12,128,128]{3,2,1,0:T(8,128)} %constant_dynamic-slice_fusion.5), channel_id=1, source_target_pairs={{0,2},{2,4},{4,6},{6,8},{8,10},{10,12},{12,14},{14,16},{16,18},{18... | collective-permute-start | bytes 9437192 | tf_op jit(solution)/shard_map/ppermute | solution.py:12
  542.6 205.9 %collective-permute-start.10 = (f32[4,12,128,128]{3,2,1,0:T(8,128)}, f32[4,12,128,128]{3,2,1,0:T(8,128)}, u32[]{:S(2)}, u32[]{:S(2)}) collective-permute-start(f32[4,12,128,128]{3,2,1,0:T(8,128)} %constant_dynamic-slice_fusion.5), channel_id=1, source_target_pairs={{0,30},{2,0},{4,2},{6,4},{8,6},{10,8},{12,10},{14,12},{16,14},{18,... | collective-permute-start | bytes 9437192 | tf_op jit(solution)/shard_map/ppermute | solution.py:12
  546.5 204.1 %collective-permute-start.11 = (f32[4,12,128,128]{3,2,1,0:T(8,128)}, f32[4,12,128,128]{3,2,1,0:T(8,128)}, u32[]{:S(2)}, u32[]{:S(2)}) collective-permute-start(f32[4,12,128,128]{3,2,1,0:T(8,128)} %constant_dynamic-slice_fusion.5), channel_id=1, source_target_pairs={{0,28},{2,30},{4,0},{6,2},{8,4},{10,6},{12,8},{14,10},{16,12},{18,... | collective-permute-start | bytes 9437192 | tf_op jit(solution)/shard_map/ppermute | solution.py:12
  548.4 199.7 %slice-start = ((s8[6291456]{0:T(1024)(128)(4,1)}), s8[4194304]{0:T(1024)(128)(4,1)S(1)}, s32[]{:S(2)}) async-start(s8[6291456]{0:T(1024)(128)(4,1)} %bitcast.115), calls=%async_computation.2 | async-start | bytes 8388608
  548.7 199.3 %slice-start.1 = ((s8[6291456]{0:T(1024)(128)(4,1)}), s8[2097152]{0:T(1024)(128)(4,1)S(1)}, s32[]{:S(2)}) async-start(s8[6291456]{0:T(1024)(128)(4,1)} %bitcast.115), calls=%async_computation.3 | async-start | bytes 4194304
  752.7 7.3 copy-start
Sparse Core Ops, SparseCore 0:
  495.4 40.5 all-reduce.5
  1021.7 34.6 all-reduce.7
where the time goes:
time: 1070 us
  waiting for transfers between devices  538 us (50%)
  local copies, waits for them, and re-layouts  276 us (26%)
  matrix products  215 us (20%)
  starting transfers between devices  19.7 us (2%)
  between operations  14.9 us (1%)
    ppermute x12, waiting for transfers between devices, passed_along(): lax.ppermute(array, axis, [(i, (i + by) % devices) for i in range(devices)])  464 us
    dot_general x4, matrix products, metric_row(): jnp.einsum('tba,tybc->tyac', factor_here, product_here, precision=HIGHEST)  95.2 us
    unnamed x4, waiting for transfers between devices  74.1 us
    dot_general x4, matrix products, product_row(): jnp.einsum('kab,kmbc->kmac', margin_row, picked, precision=HIGHEST)  70.2 us
    transpose x4, local copies, waits for them, and re-layouts, metric_row(): jnp.einsum('tba,tybc->tyac', factor_here, product_here, precision=HIGHEST)  51 us
    gather x4, local copies, waits for them, and re-layouts, product_row(): picked = halo_factor[relative_row]  45.6 us
    gather x4, local copies, waits for them, and re-layouts, metric_row(): product_here = halo_product[source_rows]  45.3 us
    transpose x4, local copies, waits for them, and re-layouts, product_row(): jnp.einsum('kab,kmbc->kmac', margin_row, picked, precision=HIGHEST)  37.2 us
  transfers between devices with their start and end apart: 14, of which 7 were waited for; matrix products, arithmetic and copies ran while one was open for 2% of the time, Pallas kernels for 0%

commit v1 on v0

v1 whole, which is shorter than its diff:
```python
import jax
import jax.numpy as jnp
from jax import lax
from jax.experimental import pallas as pl
from jax.experimental.pallas import tpu as pltpu
from jax.sharding import PartitionSpec as P

GROUP = 4
CODE = 1024


def flip_x(s, n):
    return s ^ 1


def flip_y(s, n):
    return s ^ 2


def step_z(s, n):
    return (s + 4) % n if s % 4 < 2 else (s - 4) % n


def hop(array, target, among=(0, 1, 2, 3)):
    n = lax.axis_size("rows")
    return lax.ppermute(array, "rows", [(s, target(s, n)) for s in range(n) if s % 4 in among])


def swap(array):
    return lax.ppermute(array, "rep", [(0, 1), (1, 0)])


def halo(chunks, inner):
    over_x = [hop(c, flip_x) for c in chunks]
    over_y = [hop(c, flip_y) for c in chunks]
    over_z = [hop(c, step_z) for c in over_y]
    second = []
    for y, z in zip(over_y, over_z):
        early = hop(y, flip_x, (0, 3))
        late = hop(z, flip_x, (1, 2))
        second.append(jnp.where(inner, early, late))
    return [over_x, over_y, over_z, second]


def block_products(table, groups, sources, moves, lhs_parts, pool_blocks, transposed, outs):
    rows, block = lhs_parts[0].shape[0], lhs_parts[0].shape[2]
    slots = sum(part.shape[1] for part in lhs_parts)
    source_count, part_count = len(sources), len(lhs_parts)

    def kernel(*refs):
        groups_ref, table_ref = refs[:2]
        source_refs = refs[2 : 2 + source_count]
        lhs_refs = refs[2 + source_count : 2 + source_count + part_count]
        out_ref, pool, high, low, sems = refs[2 + source_count + part_count :]
        copies = []
        for index, (source, at, dst, count) in enumerate(moves):
            copy = pltpu.make_async_copy(
                source_refs[source].at[at], pool.at[pl.ds(dst, count)], sems.at[index]
            )
            copy.start()
            copies.append(copy)
        pool[pool_blocks] = jnp.zeros((block, block), jnp.float32)

        def split_row(row, carry):
            base = row * slots
            for ref in lhs_refs:
                for s in range(ref.shape[1]):
                    value = ref[row, s]
                    if transposed:
                        value = value.T
                    top = value.astype(jnp.bfloat16)
                    high[base + s] = top
                    low[base + s] = (value - top.astype(jnp.float32)).astype(jnp.bfloat16)
                base = base + ref.shape[1]
            return carry

        lax.fori_loop(0, rows, split_row, 0)
        for copy in copies:
            copy.wait()

        def one_output(o, carry):
            row = o // outs

            def one_group(g, total):
                left, right = [], []
                for e in range(GROUP):
                    code = table_ref[o * slots + g * GROUP + e]
                    s = row * slots + code // CODE
                    value = pool[code % CODE]
                    top = value.astype(jnp.bfloat16)
                    rest = (value - top.astype(jnp.float32)).astype(jnp.bfloat16)
                    left += [high[s], high[s], low[s]]
                    right += [top, rest, top]
                return total + jnp.dot(
                    jnp.concatenate(left, axis=1),
                    jnp.concatenate(right, axis=0),
                    preferred_element_type=jnp.float32,
                )

            out_ref[o] = lax.fori_loop(
                0, groups_ref[o], one_group, jnp.zeros((block, block), jnp.float32)
            )
            return carry

        lax.fori_loop(0, rows * outs, one_output, 0)

    in_specs = (
        [pl.BlockSpec(memory_space=pltpu.SMEM)] * 2
        + [pl.BlockSpec(memory_space=pl.ANY)] * source_count
        + [pl.BlockSpec(memory_space=pltpu.VMEM)] * part_count
    )
    result = pl.pallas_call(
        kernel,
        out_shape=jax.ShapeDtypeStruct((rows * outs, block, block), jnp.float32),
        in_specs=in_specs,
        out_specs=pl.BlockSpec(memory_space=pltpu.VMEM),
        scratch_shapes=[
            pltpu.VMEM((pool_blocks + 1, block, block), jnp.float32),
            pltpu.VMEM((rows * slots, block, block), jnp.bfloat16),
            pltpu.VMEM((rows * slots, block, block), jnp.bfloat16),
            pltpu.SemaphoreType.DMA((len(moves),)),
        ],
        compiler_params=pltpu.CompilerParams(vmem_limit_bytes=52 * 1024 * 1024),
        cost_estimate=pl.CostEstimate(
            flops=rows * outs * 10 * 6 * block**3 * 4,
            bytes_accessed=(pool_blocks + rows * (slots + outs)) * block * block * 4,
            transcendentals=0,
        ),
    )(groups.reshape(-1), table.reshape(-1), *sources, *lhs_parts)
    return result.reshape(rows, outs, block, block)


def packed_list(found, codes, dummy):
    slots = found.shape[-1]
    index = jnp.arange(slots, dtype=jnp.int32)
    before = (index[:, None] > index[None, :]).astype(jnp.int32)
    rank = jnp.sum(found[..., None, :] * before, axis=-1)
    count = jnp.sum(found, axis=-1)
    chosen = found[..., None, :] * (rank[..., None, :] == index[:, None]).astype(jnp.int32)
    listed = jnp.sum(chosen * codes[..., None, :], axis=-1)
    listed = jnp.where(index < count[..., None], listed, dummy)
    return listed, (count + GROUP - 1) // GROUP


def shards(margin_blocks, margin_cols, factor_blocks, factor_cols, product_cols, metric_cols):
    rows, slots, block = factor_blocks.shape[:3]
    kept, kept_x = product_cols.shape[1], metric_cols.shape[1]
    half_rows, half_kept, half_x = rows // 2, kept // 2, kept_x // 2
    n = lax.axis_size("rows")
    r = lax.axis_index("rows")
    q = lax.axis_index("rep")
    place = r % 4
    inner = (place == 1) | (place == 2)
    int32 = jnp.int32

    mine = lax.dynamic_slice_in_dim(factor_blocks, q * half_rows, half_rows, 0)
    near = halo([mine[c] for c in range(half_rows)], inner)
    their_margin = swap(margin_blocks)
    near_theirs = [[swap(c) for c in chunks] for chunks in near]

    sign_x = 1 - 2 * (place % 2)
    sign_y = 2 - 4 * (place // 2)
    patterns = jnp.concatenate([factor_cols, product_cols], axis=1)
    by_offset = [
        lax.ppermute(patterns, "rows", [(s, (s - o) % n) for s in range(n)]) if o else patterns
        for o in (-2, -1, 0, 1, 2)
    ]
    offsets = jnp.stack([0 * sign_x, sign_x, sign_y, -sign_y, -sign_x]).astype(int32)
    which = (offsets[:, None] == jnp.arange(-2, 3, dtype=int32)[None, :]).astype(int32)
    near_patterns = jnp.sum(which[:, :, None, None] * jnp.stack(by_offset)[None], axis=1)
    near_patterns = near_patterns.reshape(5 * rows, slots + kept)
    near_factor_cols = near_patterns[:, :slots]
    near_product_cols = near_patterns[:, slots:]
    near_index = jnp.arange(5 * rows, dtype=int32)
    row_of, slot_of = near_index % rows, near_index // rows
    swapped = slot_of * rows + ((row_of // half_rows) ^ q) * half_rows + row_of % half_rows
    factor_at = jnp.where(slot_of == 0, near_index, swapped).astype(int32)

    columns = jnp.concatenate([margin_cols, swap(margin_cols)], axis=1)
    offset = (columns // rows - r + 2) % n - 2
    slot = jnp.sum((offset[..., None] == offsets) * jnp.arange(5, dtype=int32), axis=-1)
    picked = (slot * rows + columns % rows)[..., None] == near_index
    picked = picked.astype(int32)
    picked_cols = jnp.sum(picked[..., None] * near_factor_cols, axis=2)
    picked_at = jnp.sum(picked * factor_at, axis=2)
    my_product_cols = lax.dynamic_slice_in_dim(product_cols, q * half_kept, half_kept, 1)
    match = (picked_cols[:, None] == my_product_cols[:, :, None, None]).astype(int32)
    m_index = jnp.arange(slots, dtype=int32)
    k_index = jnp.arange(columns.shape[1], dtype=int32)
    code = k_index[:, None] * CODE + picked_at[:, None, :, None] * slots + m_index
    table, groups = packed_list(
        jnp.sum(match, axis=-1), jnp.sum(match * code, axis=-1), 5 * rows * slots
    )

    sources, moves = [factor_blocks], []
    for row in range(rows):
        moves.append((0, row, row * slots, slots))
    for j in range(4):
        for h, chunks in enumerate((near[j], near_theirs[j])):
            for c, chunk in enumerate(chunks):
                dst = ((j + 1) * rows + h * half_rows + c) * slots
                moves.append((len(sources), slice(None), dst, slots))
                sources.append(chunk)
    product = block_products(
        table,
        groups,
        sources,
        moves,
        [margin_blocks, their_margin],
        5 * rows * slots,
        False,
        half_kept,
    )

    chunks = [product[:half_rows], product[half_rows:]]
    near_product = [chunks] + halo(chunks, inner)
    near_product_theirs = [[swap(c) for c in part] for part in near_product]

    targets = r * rows + jnp.arange(rows, dtype=int32)
    hit = (near_factor_cols[None] == targets[:, None, None]).astype(int32)
    held = jnp.sum(hit, axis=-1)
    at = jnp.sum(hit * (factor_at[:, None] * slots + m_index), axis=-1)
    entry_code, _ = packed_list(held, near_index * (5 * rows * slots) + at, 0)
    entry_code = entry_code[:, :slots]
    entry_row = entry_code // (5 * rows * slots)
    entry_at = entry_code % (5 * rows * slots)
    flat = jnp.concatenate(
        [factor_blocks.reshape(-1, block, block)]
        + [c for j in range(4) for part in (near[j], near_theirs[j]) for c in part]
    )
    entries = flat[entry_at]
    order = jnp.where(q == 0, near_product_cols, jnp.roll(near_product_cols, half_kept, axis=1))
    entry_pick = (entry_row[..., None] == near_index).astype(int32)
    entry_cols = jnp.sum(entry_pick[..., None] * order, axis=2)
    my_metric_cols = lax.dynamic_slice_in_dim(metric_cols, q * half_x, half_x, 1)
    match = (entry_cols[:, None] == my_metric_cols[:, :, None, None]).astype(int32)
    y_index = jnp.arange(kept, dtype=int32)
    code = m_index[:, None] * CODE + entry_row[:, None, :, None] * kept + y_index
    table, groups = packed_list(
        jnp.sum(match, axis=-1), jnp.sum(match * code, axis=-1), 5 * rows * kept
    )

    sources, moves = [], []
    for j in range(5):
        for h, parts in enumerate((near_product[j], near_product_theirs[j])):
            for c, chunk in enumerate(parts):
                for row in range(half_rows):
                    dst = (j * rows + c * half_rows + row) * kept + h * half_kept
                    moves.append((len(sources), row, dst, half_kept))
                sources.append(chunk)
    metric = block_products(
        table, groups, sources, moves, [entries], 5 * rows * kept, True, half_x
    )
    return (product, metric)


def solution(mesh):
    return jax.shard_map(
        shards,
        mesh=mesh,
        in_specs=(
            P("rows", "rep", None, None),
            P("rows", "rep"),
            P("rows", None, None, None),
            P("rows", None),
            P("rows", None),
            P("rows", None),
        ),
        out_specs=(P("rows", "rep", None, None), P("rows", "rep", None, None)),
        check_vma=False,
    )
```

time: 1070 us -> 479 us (0.45)
  waiting for transfers between devices: 538 us -> 252 us
  local copies, waits for them, and re-layouts: 276 us -> 42.1 us
  matrix products: 215 us -> 0 us
  Pallas kernels: 0 us -> 89 us
  starting transfers between devices: 19.7 us -> 70 us
  other arithmetic: 3.33 us -> 19.5 us
  between operations: 14.9 us -> 1.3 us
    dot_general x16 -> x0, matrix products: 215 us -> none  [the longest x4 95.2 us: metric_row(): jnp.einsum('tba,tybc->tyac', factor_here, product_here, precision=HIGHEST)]
    ppermute x12 -> x44, waiting for transfers between devices: 464 us -> 252 us  [the longest x20 206 us: hop(): lax.ppermute(array, 'rows', [(s, target(s, n)) for s in range(n) if s % 4...]
    gather x24 -> x1, local copies, waits for them, and re-layouts: 126 us -> 9.76 us  [shards(): entries = flat[entry_at]]
    pallas_call x0 -> x2, Pallas kernels: none -> 89 us  [block_products(): pl.pallas_call(kernel, out_shape=jax.ShapeDtypeStruct((rows * outs, block...]
    transpose x8 -> x0, local copies, waits for them, and re-layouts: 88.2 us -> none  [the longest x4 51 us: metric_row(): jnp.einsum('tba,tybc->tyac', factor_here, product_here, precision=HIGHEST)]
    unnamed x4 -> x0, waiting for transfers between devices: 74.1 us -> none
    ppermute x12 -> x44, starting transfers between devices: 19.5 us -> 70 us  [the longest x20 35.8 us: swap(): return lax.ppermute(array, 'rep', [(0, 1), (1, 0)])]
    dynamic_update_slice x8 -> x0, local copies, waits for them, and re-layouts: 11.7 us -> none  [shards(): lax.map(product_row, (margin_blocks, relative, product_cols))]
  transfers between devices with their start and end apart: 14 -> 44, of which waited for: 7 -> 18; matrix products, arithmetic and copies ran while one was open for 2% -> 12% of each run, Pallas kernels for 0% -> 0%
where the time goes in v1:
time: 479 us; the launch traced here: 474 us
  waiting for transfers between devices  252 us (53%)
  Pallas kernels  89 us (19%)
  starting transfers between devices  70 us (15%)
  local copies, waits for them, and re-layouts  42.1 us (9%)
  other arithmetic  19.5 us (4%)
    ppermute x20, waiting for transfers between devices, hop(): lax.ppermute(array, 'rows', [(s, target(s, n)) for s in range(n) if s % 4...  206 us
    pallas_call x2, Pallas kernels, block_products(): pl.pallas_call(kernel, out_shape=jax.ShapeDtypeStruct((rows * outs, block...  89 us
    ppermute x4, waiting for transfers between devices, shards(): lax.ppermute(patterns, 'rows', [(s, (s - o) % n) for s in range(n)])  39.8 us
    ppermute x20, starting transfers between devices, swap(): return lax.ppermute(array, 'rep', [(0, 1), (1, 0)])  35.8 us
    ppermute x20, starting transfers between devices, hop(): lax.ppermute(array, 'rows', [(s, target(s, n)) for s in range(n) if s % 4...  28.2 us
    unnamed x60, local copies, waits for them, and re-layouts  24.6 us
    gather x1, local copies, waits for them, and re-layouts, shards(): entries = flat[entry_at]  9.76 us
  transfers between devices with their start and end apart: 44, of which 18 were waited for; matrix products, arithmetic and copies ran while one was open for 12% of the time, Pallas kernels for 0%

profile of v1, /device:TPU:1, one launch (start us, length us, event | category | flops | bytes accessed | tf_op | source)
XLA Modules:
  0.0 473.6 jit_solution(926984351834378754)
XLA Ops:
  0.7 1.7 dynamic-slice_bitcast_fusion
  2.3 2.1 collective-permute-start.5
  6.0 1.5 collective-permute-start
  7.6 4.7 constant_dynamic-update-slice_fusion.21
  14.0 1.7 collective-permute-start.1
  17.6 32.1 %collective-permute-done.1 = s32[4,40]{1,0:T(4,128)S(1)} collective-permute-done((s32[4,40]{1,0:T(4,128)S(1)}, s32[4,40]{1,0:T(4,128)S(1)}, u32[]{:S(2)}, u32[]{:S(2)}) %collective-permute-start.1) | collective-permute-done | bytes 672 | tf_op jit(solution)/shard_map/ppermute | solution.py:165
  50.0 6.0 %collective-permute-done.2 = s32[4,40]{1,0:T(4,128)S(1)} collective-permute-done((s32[4,40]{1,0:T(4,128)S(1)}, s32[4,40]{1,0:T(4,128)S(1)}, u32[]{:S(2)}, u32[]{:S(2)}) %collective-permute-start.2) | collective-permute-done | bytes 672 | tf_op jit(solution)/shard_map/ppermute | solution.py:165
  56.0 1.5 collective-permute-start.3
  58.4 2.6 collective-permute-start.4
  63.3 4.9 %collective-permute-start.7 = (f32[16,128,128]{2,1,0:T(8,128)S(1)}, f32[16,128,128]{2,1,0:T(8,128)S(1)}, u32[]{:S(2)}, u32[]{:S(2)}) collective-permute-start(f32[16,128,128]{2,1,0:T(8,128)S(1)} %collective-permute-done.5.refs_3_), channel_id=1, source_target_pairs={{0,1},{1,0},{2,3},{3,2},{4,5},{5,4},{6,7},{7,6},{8,9},{9,8},{10,11... | collective-permute-start | bytes 3145736 | tf_op jit(solution)/shard_map/ppermute | solution.py:30
  70.8 2.6 convert_reduce_fusion
  74.0 21.0 %collective-permute-done.13.refs_11_ = f32[16,128,128]{2,1,0:T(8,128)S(1)} collective-permute-done((f32[16,128,128]{2,1,0:T(8,128)}, f32[16,128,128]{2,1,0:T(8,128)S(1)}, u32[]{:S(2)}, u32[]{:S(2)}) %collective-permute-start.13) | collective-permute-done | bytes 1048608 | tf_op jit(solution)/shard_map/ppermute | solution.py:26
  97.4 20.0 %collective-permute-done.14.refs_12_ = f32[16,128,128]{2,1,0:T(8,128)S(1)} collective-permute-done((f32[16,128,128]{2,1,0:T(8,128)}, f32[16,128,128]{2,1,0:T(8,128)S(1)}, u32[]{:S(2)}, u32[]{:S(2)}) %collective-permute-start.14) | collective-permute-done | bytes 1048608 | tf_op jit(solution)/shard_map/ppermute | solution.py:26
  118.3 2.3 constant_dynamic-update-slice_fusion.19
  121.7 4.9 %collective-permute-start.17 = (f32[16,128,128]{2,1,0:T(8,128)}, f32[16,128,128]{2,1,0:T(8,128)S(1)}, u32[]{:S(2)}, u32[]{:S(2)}) collective-permute-start(f32[16,128,128]{2,1,0:T(8,128)} %collective-permute-done.9.refs_7_), channel_id=1, source_target_pairs={{0,2},{6,4},{8,10},{14,12},{16,18},{22,20},{24,26},{30,28},{1,3},{... | collective-permute-start | bytes 3145736 | tf_op jit(solution)/shard_map/ppermute | solution.py:26
  129.1 2.4 constant_dynamic-update-slice_fusion.16
  131.5 2.3 constant_dynamic-update-slice_fusion.15
  133.8 4.1 collective-permute-start.19
  137.9 1.5 collective-permute-start.20
  147.1 2.0 collective-permute-done.17
  149.0 4.7 collective-permute-done.18
  154.9 2.7 collective-permute-start.21
  157.6 13.9 %collective-permute-done.19 = f32[16,128,128]{2,1,0:T(8,128)S(1)} collective-permute-done((f32[16,128,128]{2,1,0:T(8,128)}, f32[16,128,128]{2,1,0:T(8,128)S(1)}, u32[]{:S(2)}, u32[]{:S(2)}) %collective-permute-start.19) | collective-permute-done | bytes 1048608 | tf_op jit(solution)/shard_map/ppermute | solution.py:26
  171.5 4.7 collective-permute-done.20
  177.4 1.5 collective-permute-start.22
  178.9 2.6 convert_reduce_fusion.2
  181.5 1.7 multiply_reduce_fusion.3
  183.2 1.7 multiply_reduce_fusion.2
  185.3 38.7 %shard_map.77 = f32[48,128,128]{2,1,0:T(8,128)} custom-call(s32[48]{0:T(128)S(1)} %and_select_fusion.5.refs_0_, s32[768]{0:T(1024)S(1)} %select_n.199.refs_1_, f32[4,16,128,128]{3,2,1,0:T(8,128)} %refs_2_.1, f32[16,128,128]{2,1,0:T(8,128)S(1)} %collective-permute-done.5.refs_3_, f32[16,128,128]{2,1,0:T(8,128)} %collective-permute-done.6.refs_4_, ...), custom_call_target="tpu_custom_call" | custom-call | flops 24159191040 | bytes 28311552 | tf_op jit(solution)/shard_map/pallas_call | solution.py:112
  224.0 2.1 fusion.18
  226.2 1.5 collective-permute-start.30
  227.7 1.7 collective-permute-start.26
  229.3 28.9 %collective-permute-done.31.refs_11_ = f32[2,12,128,128]{3,2,1,0:T(8,128)} collective-permute-done((f32[2,12,128,128]{3,2,1,0:T(8,128)S(1)}, f32[2,12,128,128]{3,2,1,0:T(8,128)}, u32[]{:S(2)}, u32[]{:S(2)}) %collective-permute-start.31) | collective-permute-done | bytes 1572896 | tf_op jit(solution)/shard_map/ppermute | solution.py:26
  258.2 33.7 %collective-permute-done.30.refs_10_ = f32[2,12,128,128]{3,2,1,0:T(8,128)S(1)} collective-permute-done((f32[2,12,128,128]{3,2,1,0:T(8,128)S(1)}, f32[2,12,128,128]{3,2,1,0:T(8,128)S(1)}, u32[]{:S(2)}, u32[]{:S(2)}) %collective-permute-start.30) | collective-permute-done | bytes 1572896 | tf_op jit(solution)/shard_map/ppermute | solution.py:26
  292.0 3.4 collective-permute-start.27
  295.4 2.0 collective-permute-start.40
  297.4 1.4 collective-permute-start.38
  300.1 25.3 %collective-permute-done.34.refs_14_ = f32[2,12,128,128]{3,2,1,0:T(8,128)} collective-permute-done((f32[2,12,128,128]{3,2,1,0:T(8,128)S(1)}, f32[2,12,128,128]{3,2,1,0:T(8,128)}, u32[]{:S(2)}, u32[]{:S(2)}) %collective-permute-start.34) | collective-permute-done | bytes 1572896 | tf_op jit(solution)/shard_map/ppermute | solution.py:26
  327.1 7.0 %collective-permute-start.24 = (f32[2,12,128,128]{3,2,1,0:T(8,128)S(1)}, f32[2,12,128,128]{3,2,1,0:T(8,128)S(1)}, u32[]{:S(2)}, u32[]{:S(2)}) collective-permute-start(f32[2,12,128,128]{3,2,1,0:T(8,128)S(1)} %bitcast.27), channel_id=1, source_target_pairs={{0,1},{1,0},{2,3},{3,2},{4,5},{5,4},{6,7},{7,6},{8,9},{9,8},{10,11... | collective-permute-start | bytes 4718600 | tf_op jit(solution)/shard_map/ppermute | solution.py:30
  334.1 25.8 %collective-permute-done.40 = f32[2,12,128,128]{3,2,1,0:T(8,128)S(1)} collective-permute-done((f32[2,12,128,128]{3,2,1,0:T(8,128)}, f32[2,12,128,128]{3,2,1,0:T(8,128)S(1)}, u32[]{:S(2)}, u32[]{:S(2)}) %collective-permute-start.40) | collective-permute-done | bytes 1572896 | tf_op jit(solution)/shard_map/ppermute | solution.py:26
  359.9 7.5 %collective-permute-start.25 = (f32[2,12,128,128]{3,2,1,0:T(8,128)S(1)}, f32[2,12,128,128]{3,2,1,0:T(8,128)S(1)}, u32[]{:S(2)}, u32[]{:S(2)}) collective-permute-start(f32[2,12,128,128]{3,2,1,0:T(8,128)S(1)} %bitcast.34), channel_id=1, source_target_pairs={{0,1},{1,0},{2,3},{3,2},{4,5},{5,4},{6,7},{7,6},{8,9},{9,8},{10,11... | collective-permute-start | bytes 4718600 | tf_op jit(solution)/shard_map/ppermute | solution.py:30
  367.3 26.1 %collective-permute-done.38 = f32[2,12,128,128]{3,2,1,0:T(8,128)S(1)} collective-permute-done((f32[2,12,128,128]{3,2,1,0:T(8,128)S(1)}, f32[2,12,128,128]{3,2,1,0:T(8,128)S(1)}, u32[]{:S(2)}, u32[]{:S(2)}) %collective-permute-start.38) | collective-permute-done | bytes 1572896 | tf_op jit(solution)/shard_map/ppermute | solution.py:26
  393.5 3.9 collective-permute-start.28
  403.1 4.1 collective-permute-done.32.refs_12_
  408.7 2.3 constant_dynamic-update-slice_fusion.6
  411.0 2.3 constant_dynamic-update-slice_fusion.5
  413.3 9.8 %gather_fusion = f32[64,128,128]{2,1,0:T(8,128)} fusion(f32[320,128,128]{2,1,0:T(8,128)} %constant_dynamic-update-slice_fusion.5, s32[1024]{0:T(1024)S(1)} %pad_clamp_fusion), kind=kCustom, calls=%fused_computation | custom fusion | bytes 8388864 | tf_op jit(solution)/shard_map/gather | solution.py:231
  423.1 50.3 %shard_map.78 = f32[48,128,128]{2,1,0:T(8,128)} custom-call(s32[48]{0:T(128)S(1)} %and_select_fusion.refs_0_, s32[768]{0:T(1024)S(1)} %select_n.210.refs_1_, f32[2,12,128,128]{3,2,1,0:T(8,128)S(1)} %bitcast.28, f32[2,12,128,128]{3,2,1,0:T(8,128)} %bitcast.35, f32[2,12,128,128]{3,2,1,0:T(8,128)} %copy-done.16, f32[2,12,128,128]{3,2,1,0:T(8,128)} %copy-done.17, ...), custom_call_target="tpu_custom_call" | custom-call | flops 24159191040 | bytes 38797312 | tf_op jit(solution)/shard_map/pallas_call | solution.py:112
  (164 shorter events, 39.3 us)
Async XLA Ops:
  2.3 61.0 %collective-permute-start.5 = (f32[16,128,128]{2,1,0:T(8,128)S(1)}, f32[16,128,128]{2,1,0:T(8,128)S(1)}, u32[]{:S(2)}, u32[]{:S(2)}) collective-permute-start(f32[16,128,128]{2,1,0:T(8,128)S(1)} %get-tuple-element.20), channel_id=1, source_target_pairs={{0,2},{2,0},{4,6},{6,4},{8,10},{10,8},{12,14},{14,12},{16,18},{18,... | collective-permute-start | bytes 3145736 | tf_op jit(solution)/shard_map/ppermute | solution.py:26
  4.4 63.8 %collective-permute-start.9 = (f32[16,128,128]{2,1,0:T(8,128)S(1)}, f32[16,128,128]{2,1,0:T(8,128)}, u32[]{:S(2)}, u32[]{:S(2)}) collective-permute-start(f32[16,128,128]{2,1,0:T(8,128)S(1)} %get-tuple-element.20), channel_id=1, source_target_pairs={{0,4},{2,6},{4,0},{6,2},{8,12},{10,14},{12,8},{14,10},{16,20},{18,... | collective-permute-start | bytes 3145736 | tf_op jit(solution)/shard_map/ppermute | solution.py:26
  5.7 62.9 %collective-permute-start.6 = (f32[16,128,128]{2,1,0:T(8,128)S(1)}, f32[16,128,128]{2,1,0:T(8,128)}, u32[]{:S(2)}, u32[]{:S(2)}) collective-permute-start(f32[16,128,128]{2,1,0:T(8,128)S(1)} %get-tuple-element.19), channel_id=1, source_target_pairs={{0,2},{2,0},{4,6},{6,4},{8,10},{10,8},{12,14},{14,12},{16,18},{18,... | collective-permute-start | bytes 3145736 | tf_op jit(solution)/shard_map/ppermute | solution.py:26
  5.9 62.4 %collective-permute-start.10 = (f32[16,128,128]{2,1,0:T(8,128)S(1)}, f32[16,128,128]{2,1,0:T(8,128)}, u32[]{:S(2)}, u32[]{:S(2)}) collective-permute-start(f32[16,128,128]{2,1,0:T(8,128)S(1)} %get-tuple-element.19), channel_id=1, source_target_pairs={{0,4},{2,6},{4,0},{6,2},{8,12},{10,14},{12,8},{14,10},{16,20},{18,... | collective-permute-start | bytes 3145736 | tf_op jit(solution)/shard_map/ppermute | solution.py:26
  6.0 8.0 %collective-permute-start = (s32[4,8]{1,0:T(4,128)}, s32[4,8]{1,0:T(4,128)S(1)}, u32[]{:S(2)}, u32[]{:S(2)}) collective-permute-start(s32[4,8]{1,0:T(4,128)} %param.7), channel_id=1, source_target_pairs={{0,1},{1,0},{2,3},{3,2},{4,5},{5,4},{6,7},{7,6},{8,9},{9,8},{10,11... | collective-permute-start | bytes 392 | tf_op jit(solution)/shard_map/ppermute | solution.py:30
  14.0 35.7 %collective-permute-start.1 = (s32[4,40]{1,0:T(4,128)S(1)}, s32[4,40]{1,0:T(4,128)S(1)}, u32[]{:S(2)}, u32[]{:S(2)}) collective-permute-start(s32[4,40]{1,0:T(4,128)S(1)} %pad_add_fusion.1), channel_id=1, source_target_pairs={{0,4},{2,6},{4,8},{6,10},{8,12},{10,14},{12,16},{14,18},{16,20},{1... | collective-permute-start | bytes 1928 | tf_op jit(solution)/shard_map/ppermute | solution.py:165
  49.7 6.3 %collective-permute-start.2 = (s32[4,40]{1,0:T(4,128)S(1)}, s32[4,40]{1,0:T(4,128)S(1)}, u32[]{:S(2)}, u32[]{:S(2)}) collective-permute-start(s32[4,40]{1,0:T(4,128)S(1)} %pad_add_fusion.1), channel_id=1, source_target_pairs={{0,2},{2,4},{4,6},{6,8},{8,10},{10,12},{12,14},{14,16},{16,18},{18... | collective-permute-start | bytes 1928 | tf_op jit(solution)/shard_map/ppermute | solution.py:165
  56.0 2.4 collective-permute-start.3
  58.4 3.3 collective-permute-start.4
  63.3 10.1 %collective-permute-start.7 = (f32[16,128,128]{2,1,0:T(8,128)S(1)}, f32[16,128,128]{2,1,0:T(8,128)S(1)}, u32[]{:S(2)}, u32[]{:S(2)}) collective-permute-start(f32[16,128,128]{2,1,0:T(8,128)S(1)} %collective-permute-done.5.refs_3_), channel_id=1, source_target_pairs={{0,1},{1,0},{2,3},{3,2},{4,5},{5,4},{6,7},{7,6},{8,9},{9,8},{10,11... | collective-permute-start | bytes 3145736 | tf_op jit(solution)/shard_map/ppermute | solution.py:30
  68.2 26.7 %collective-permute-start.13 = (f32[16,128,128]{2,1,0:T(8,128)}, f32[16,128,128]{2,1,0:T(8,128)S(1)}, u32[]{:S(2)}, u32[]{:S(2)}) collective-permute-start(f32[16,128,128]{2,1,0:T(8,128)} %collective-permute-done.9.refs_7_), channel_id=1, source_target_pairs={{0,8},{2,10},{4,28},{6,30},{8,16},{10,18},{12,4},{14,6},{16,24},{1... | collective-permute-start | bytes 3145736 | tf_op jit(solution)/shard_map/ppermute | solution.py:26
  68.3 49.1 %collective-permute-start.14 = (f32[16,128,128]{2,1,0:T(8,128)}, f32[16,128,128]{2,1,0:T(8,128)S(1)}, u32[]{:S(2)}, u32[]{:S(2)}) collective-permute-start(f32[16,128,128]{2,1,0:T(8,128)} %collective-permute-done.10.refs_8_), channel_id=1, source_target_pairs={{0,8},{2,10},{4,28},{6,30},{8,16},{10,18},{12,4},{14,6},{16,24},{1... | collective-permute-start | bytes 3145736 | tf_op jit(solution)/shard_map/ppermute | solution.py:26
  68.6 53.2 %collective-permute-start.8 = (f32[16,128,128]{2,1,0:T(8,128)}, f32[16,128,128]{2,1,0:T(8,128)S(1)}, u32[]{:S(2)}, u32[]{:S(2)}) collective-permute-start(f32[16,128,128]{2,1,0:T(8,128)} %collective-permute-done.6.refs_4_), channel_id=1, source_target_pairs={{0,1},{1,0},{2,3},{3,2},{4,5},{5,4},{6,7},{7,6},{8,9},{9,8},{10,11... | collective-permute-start | bytes 3145736 | tf_op jit(solution)/shard_map/ppermute | solution.py:30
  69.3 58.5 %collective-permute-start.11 = (f32[16,128,128]{2,1,0:T(8,128)}, f32[16,128,128]{2,1,0:T(8,128)S(1)}, u32[]{:S(2)}, u32[]{:S(2)}) collective-permute-start(f32[16,128,128]{2,1,0:T(8,128)} %collective-permute-done.9.refs_7_), channel_id=1, source_target_pairs={{0,1},{1,0},{2,3},{3,2},{4,5},{5,4},{6,7},{7,6},{8,9},{9,8},{10,11... | collective-permute-start | bytes 3145736 | tf_op jit(solution)/shard_map/ppermute | solution.py:30
  73.4 60.4 %collective-permute-start.12 = (f32[16,128,128]{2,1,0:T(8,128)}, f32[16,128,128]{2,1,0:T(8,128)S(1)}, u32[]{:S(2)}, u32[]{:S(2)}) collective-permute-start(f32[16,128,128]{2,1,0:T(8,128)} %collective-permute-done.10.refs_8_), channel_id=1, source_target_pairs={{0,1},{1,0},{2,3},{3,2},{4,5},{5,4},{6,7},{7,6},{8,9},{9,8},{10,11... | collective-permute-start | bytes 3145736 | tf_op jit(solution)/shard_map/ppermute | solution.py:30
  95.0 42.9 %collective-permute-start.15 = (f32[16,128,128]{2,1,0:T(8,128)S(1)}, f32[16,128,128]{2,1,0:T(8,128)S(1)}, u32[]{:S(2)}, u32[]{:S(2)}) collective-permute-start(f32[16,128,128]{2,1,0:T(8,128)S(1)} %collective-permute-done.13.refs_11_), channel_id=1, source_target_pairs={{0,1},{1,0},{2,3},{3,2},{4,5},{5,4},{6,7},{7,6},{8,9},{9,8},{10,11... | collective-permute-start | bytes 3145736 | tf_op jit(solution)/shard_map/ppermute | solution.py:30
  117.4 25.3 %collective-permute-start.16 = (f32[16,128,128]{2,1,0:T(8,128)S(1)}, f32[16,128,128]{2,1,0:T(8,128)S(1)}, u32[]{:S(2)}, u32[]{:S(2)}) collective-permute-start(f32[16,128,128]{2,1,0:T(8,128)S(1)} %collective-permute-done.14.refs_12_), channel_id=1, source_target_pairs={{0,1},{1,0},{2,3},{3,2},{4,5},{5,4},{6,7},{7,6},{8,9},{9,8},{10,11... | collective-permute-start | bytes 3145736 | tf_op jit(solution)/shard_map/ppermute | solution.py:30
  121.7 27.3 %collective-permute-start.17 = (f32[16,128,128]{2,1,0:T(8,128)}, f32[16,128,128]{2,1,0:T(8,128)S(1)}, u32[]{:S(2)}, u32[]{:S(2)}) collective-permute-start(f32[16,128,128]{2,1,0:T(8,128)} %collective-permute-done.9.refs_7_), channel_id=1, source_target_pairs={{0,2},{6,4},{8,10},{14,12},{16,18},{22,20},{24,26},{30,28},{1,3},{... | collective-permute-start | bytes 3145736 | tf_op jit(solution)/shard_map/ppermute | solution.py:26
  127.8 25.9 %collective-permute-start.18 = (f32[16,128,128]{2,1,0:T(8,128)S(1)}, f32[16,128,128]{2,1,0:T(8,128)S(1)}, u32[]{:S(2)}, u32[]{:S(2)}) collective-permute-start(f32[16,128,128]{2,1,0:T(8,128)S(1)} %collective-permute-done.13.refs_11_), channel_id=1, source_target_pairs={{2,0},{4,6},{10,8},{12,14},{18,16},{20,22},{26,24},{28,30},{3,1},{... | collective-permute-start | bytes 3145736 | tf_op jit(solution)/shard_map/ppermute | solution.py:26
  133.8 37.7 %collective-permute-start.19 = (f32[16,128,128]{2,1,0:T(8,128)}, f32[16,128,128]{2,1,0:T(8,128)S(1)}, u32[]{:S(2)}, u32[]{:S(2)}) collective-permute-start(f32[16,128,128]{2,1,0:T(8,128)} %collective-permute-done.10.refs_8_), channel_id=1, source_target_pairs={{0,2},{6,4},{8,10},{14,12},{16,18},{22,20},{24,26},{30,28},{1,3},{... | collective-permute-start | bytes 3145736 | tf_op jit(solution)/shard_map/ppermute | solution.py:26
  137.9 38.3 %collective-permute-start.20 = (f32[16,128,128]{2,1,0:T(8,128)S(1)}, f32[16,128,128]{2,1,0:T(8,128)S(1)}, u32[]{:S(2)}, u32[]{:S(2)}) collective-permute-start(f32[16,128,128]{2,1,0:T(8,128)S(1)} %collective-permute-done.14.refs_12_), channel_id=1, source_target_pairs={{2,0},{4,6},{10,8},{12,14},{18,16},{20,22},{26,24},{28,30},{3,1},{... | collective-permute-start | bytes 3145736 | tf_op jit(solution)/shard_map/ppermute | solution.py:26
  142.7 42.6 %collective-permute-start.23 = (f32[4,8,128,128]{3,2,1,0:T(8,128)}, f32[4,8,128,128]{3,2,1,0:T(8,128)}, u32[]{:S(2)}, u32[]{:S(2)}) collective-permute-start(f32[4,8,128,128]{3,2,1,0:T(8,128)} %refs_19_.1), channel_id=1, source_target_pairs={{0,1},{1,0},{2,3},{3,2},{4,5},{5,4},{6,7},{7,6},{8,9},{9,8},{10,11... | collective-permute-start | bytes 6291464 | tf_op jit(solution)/shard_map/ppermute | solution.py:30
  154.9 30.4 %collective-permute-start.21 = (f32[16,128,128]{2,1,0:T(8,128)S(1)}, f32[16,128,128]{2,1,0:T(8,128)}, u32[]{:S(2)}, u32[]{:S(2)}) collective-permute-start(f32[16,128,128]{2,1,0:T(8,128)S(1)} %get-tuple-element.16.refs_15_), channel_id=1, source_target_pairs={{0,1},{1,0},{2,3},{3,2},{4,5},{5,4},{6,7},{7,6},{8,9},{9,8},{10,11... | collective-permute-start | bytes 3145736 | tf_op jit(solution)/shard_map/ppermute | solution.py:30
  177.4 7.9 %collective-permute-start.22 = (f32[16,128,128]{2,1,0:T(8,128)S(1)}, f32[16,128,128]{2,1,0:T(8,128)}, u32[]{:S(2)}, u32[]{:S(2)}) collective-permute-start(f32[16,128,128]{2,1,0:T(8,128)S(1)} %get-tuple-element.14.refs_16_), channel_id=1, source_target_pairs={{0,1},{1,0},{2,3},{3,2},{4,5},{5,4},{6,7},{7,6},{8,9},{9,8},{10,11... | collective-permute-start | bytes 3145736 | tf_op jit(solution)/shard_map/ppermute | solution.py:30
  226.1 174.6 %copy-start.2 = (f32[24,128,128]{2,1,0:T(8,128)}, f32[24,128,128]{2,1,0:T(8,128)S(1)}, u32[]{:S(2)}) copy-start(f32[24,128,128]{2,1,0:T(8,128)S(1)} %get-tuple-element.21) | copy-start | bytes 4718596
  226.1 32.1 %collective-permute-start.31 = (f32[2,12,128,128]{3,2,1,0:T(8,128)S(1)}, f32[2,12,128,128]{3,2,1,0:T(8,128)}, u32[]{:S(2)}, u32[]{:S(2)}) collective-permute-start(f32[2,12,128,128]{3,2,1,0:T(8,128)S(1)} %bitcast.32), channel_id=1, source_target_pairs={{0,4},{2,6},{4,0},{6,2},{8,12},{10,14},{12,8},{14,10},{16,20},{18,... | collective-permute-start | bytes 4718600 | tf_op jit(solution)/shard_map/ppermute | solution.py:26
  226.2 65.7 %collective-permute-start.30 = (f32[2,12,128,128]{3,2,1,0:T(8,128)S(1)}, f32[2,12,128,128]{3,2,1,0:T(8,128)S(1)}, u32[]{:S(2)}, u32[]{:S(2)}) collective-permute-start(f32[2,12,128,128]{3,2,1,0:T(8,128)S(1)} %bitcast.25), channel_id=1, source_target_pairs={{0,4},{2,6},{4,0},{6,2},{8,12},{10,14},{12,8},{14,10},{16,20},{18,... | collective-permute-start | bytes 4718600 | tf_op jit(solution)/shard_map/ppermute | solution.py:26
  227.7 69.7 %collective-permute-start.26 = (f32[2,12,128,128]{3,2,1,0:T(8,128)S(1)}, f32[2,12,128,128]{3,2,1,0:T(8,128)S(1)}, u32[]{:S(2)}, u32[]{:S(2)}) collective-permute-start(f32[2,12,128,128]{3,2,1,0:T(8,128)S(1)} %bitcast.26), channel_id=1, source_target_pairs={{0,2},{2,0},{4,6},{6,4},{8,10},{10,8},{12,14},{14,12},{16,18},{18,... | collective-permute-start | bytes 4718600 | tf_op jit(solution)/shard_map/ppermute | solution.py:26
  258.2 40.6 %collective-permute-start.35 = (f32[2,12,128,128]{3,2,1,0:T(8,128)}, f32[2,12,128,128]{3,2,1,0:T(8,128)}, u32[]{:S(2)}, u32[]{:S(2)}) collective-permute-start(f32[2,12,128,128]{3,2,1,0:T(8,128)} %collective-permute-done.31.refs_11_), channel_id=1, source_target_pairs={{0,8},{2,10},{4,28},{6,30},{8,16},{10,18},{12,4},{14,6},{16,24},{1... | collective-permute-start | bytes 4718600 | tf_op jit(solution)/shard_map/ppermute | solution.py:26
  291.9 115.6 %copy-start.13 = (f32[2,12,128,128]{3,2,1,0:T(8,128)}, f32[2,12,128,128]{3,2,1,0:T(8,128)S(1)}, u32[]{:S(2)}) copy-start(f32[2,12,128,128]{3,2,1,0:T(8,128)S(1)} %collective-permute-done.30.refs_10_) | copy-start | bytes 4718596
  291.9 33.4 %collective-permute-start.34 = (f32[2,12,128,128]{3,2,1,0:T(8,128)S(1)}, f32[2,12,128,128]{3,2,1,0:T(8,128)}, u32[]{:S(2)}, u32[]{:S(2)}) collective-permute-start(f32[2,12,128,128]{3,2,1,0:T(8,128)S(1)} %collective-permute-done.30.refs_10_), channel_id=1, source_target_pairs={{0,8},{2,10},{4,28},{6,30},{8,16},{10,18},{12,4},{14,6},{16,24},{1... | collective-permute-start | bytes 4718600 | tf_op jit(solution)/shard_map/ppermute | solution.py:26
  292.0 35.1 %collective-permute-start.27 = (f32[2,12,128,128]{3,2,1,0:T(8,128)S(1)}, f32[2,12,128,128]{3,2,1,0:T(8,128)S(1)}, u32[]{:S(2)}, u32[]{:S(2)}) collective-permute-start(f32[2,12,128,128]{3,2,1,0:T(8,128)S(1)} %bitcast.33), channel_id=1, source_target_pairs={{0,2},{2,0},{4,6},{6,4},{8,10},{10,8},{12,14},{14,12},{16,18},{18,... | collective-permute-start | bytes 4718600 | tf_op jit(solution)/shard_map/ppermute | solution.py:26
  295.4 64.5 %collective-permute-start.40 = (f32[2,12,128,128]{3,2,1,0:T(8,128)}, f32[2,12,128,128]{3,2,1,0:T(8,128)S(1)}, u32[]{:S(2)}, u32[]{:S(2)}) collective-permute-start(f32[2,12,128,128]{3,2,1,0:T(8,128)} %collective-permute-done.31.refs_11_), channel_id=1, source_target_pairs={{0,2},{6,4},{8,10},{14,12},{16,18},{22,20},{24,26},{30,28},{1,3},{... | collective-permute-start | bytes 4718600 | tf_op jit(solution)/shard_map/ppermute | solution.py:26
  297.4 110.2 %copy-start.14 = (f32[2,12,128,128]{3,2,1,0:T(8,128)}, f32[2,12,128,128]{3,2,1,0:T(8,128)S(1)}, u32[]{:S(2)}) copy-start(f32[2,12,128,128]{3,2,1,0:T(8,128)S(1)} %collective-permute-done.26.refs_6_) | copy-start | bytes 4718596
  297.4 96.1 %collective-permute-start.38 = (f32[2,12,128,128]{3,2,1,0:T(8,128)S(1)}, f32[2,12,128,128]{3,2,1,0:T(8,128)S(1)}, u32[]{:S(2)}, u32[]{:S(2)}) collective-permute-start(f32[2,12,128,128]{3,2,1,0:T(8,128)S(1)} %collective-permute-done.30.refs_10_), channel_id=1, source_target_pairs={{0,2},{6,4},{8,10},{14,12},{16,18},{22,20},{24,26},{30,28},{1,3},{... | collective-permute-start | bytes 4718600 | tf_op jit(solution)/shard_map/ppermute | solution.py:26
  298.8 98.6 %collective-permute-start.41 = (f32[2,12,128,128]{3,2,1,0:T(8,128)}, f32[2,12,128,128]{3,2,1,0:T(8,128)S(1)}, u32[]{:S(2)}, u32[]{:S(2)}) collective-permute-start(f32[2,12,128,128]{3,2,1,0:T(8,128)} %collective-permute-done.35.refs_15_), channel_id=1, source_target_pairs={{2,0},{4,6},{10,8},{12,14},{18,16},{20,22},{26,24},{28,30},{3,1},{... | collective-permute-start | bytes 4718600 | tf_op jit(solution)/shard_map/ppermute | solution.py:26
  325.4 72.0 %collective-permute-start.39 = (f32[2,12,128,128]{3,2,1,0:T(8,128)}, f32[2,12,128,128]{3,2,1,0:T(8,128)S(1)}, u32[]{:S(2)}, u32[]{:S(2)}) collective-permute-start(f32[2,12,128,128]{3,2,1,0:T(8,128)} %collective-permute-done.34.refs_14_), channel_id=1, source_target_pairs={{2,0},{4,6},{10,8},{12,14},{18,16},{20,22},{26,24},{28,30},{3,1},{... | collective-permute-start | bytes 4718600 | tf_op jit(solution)/shard_map/ppermute | solution.py:26
  327.1 80.5 %copy-start.15 = (f32[2,12,128,128]{3,2,1,0:T(8,128)}, f32[2,12,128,128]{3,2,1,0:T(8,128)S(1)}, u32[]{:S(2)}) copy-start(f32[2,12,128,128]{3,2,1,0:T(8,128)S(1)} %collective-permute-done.27.refs_7_) | copy-start | bytes 4718596
  327.1 73.7 %collective-permute-start.24 = (f32[2,12,128,128]{3,2,1,0:T(8,128)S(1)}, f32[2,12,128,128]{3,2,1,0:T(8,128)S(1)}, u32[]{:S(2)}, u32[]{:S(2)}) collective-permute-start(f32[2,12,128,128]{3,2,1,0:T(8,128)S(1)} %bitcast.27), channel_id=1, source_target_pairs={{0,1},{1,0},{2,3},{3,2},{4,5},{5,4},{6,7},{7,6},{8,9},{9,8},{10,11... | collective-permute-start | bytes 4718600 | tf_op jit(solution)/shard_map/ppermute | solution.py:30
  359.9 41.0 %collective-permute-start.25 = (f32[2,12,128,128]{3,2,1,0:T(8,128)S(1)}, f32[2,12,128,128]{3,2,1,0:T(8,128)S(1)}, u32[]{:S(2)}, u32[]{:S(2)}) collective-permute-start(f32[2,12,128,128]{3,2,1,0:T(8,128)S(1)} %bitcast.34), channel_id=1, source_target_pairs={{0,1},{1,0},{2,3},{3,2},{4,5},{5,4},{6,7},{7,6},{8,9},{9,8},{10,11... | collective-permute-start | bytes 4718600 | tf_op jit(solution)/shard_map/ppermute | solution.py:30
  393.5 7.9 %collective-permute-start.28 = (f32[2,12,128,128]{3,2,1,0:T(8,128)S(1)}, f32[2,12,128,128]{3,2,1,0:T(8,128)S(1)}, u32[]{:S(2)}, u32[]{:S(2)}) collective-permute-start(f32[2,12,128,128]{3,2,1,0:T(8,128)S(1)} %collective-permute-done.26.refs_6_), channel_id=1, source_target_pairs={{0,1},{1,0},{2,3},{3,2},{4,5},{5,4},{6,7},{7,6},{8,9},{9,8},{10,11... | collective-permute-start | bytes 4718600 | tf_op jit(solution)/shard_map/ppermute | solution.py:30
  397.4 5.3 %collective-permute-start.29 = (f32[2,12,128,128]{3,2,1,0:T(8,128)S(1)}, f32[2,12,128,128]{3,2,1,0:T(8,128)S(1)}, u32[]{:S(2)}, u32[]{:S(2)}) collective-permute-start(f32[2,12,128,128]{3,2,1,0:T(8,128)S(1)} %collective-permute-done.27.refs_7_), channel_id=1, source_target_pairs={{0,1},{1,0},{2,3},{3,2},{4,5},{5,4},{6,7},{7,6},{8,9},{9,8},{10,11... | collective-permute-start | bytes 4718600 | tf_op jit(solution)/shard_map/ppermute | solution.py:30
  397.4 9.8 %collective-permute-start.32 = (f32[2,12,128,128]{3,2,1,0:T(8,128)S(1)}, f32[2,12,128,128]{3,2,1,0:T(8,128)S(1)}, u32[]{:S(2)}, u32[]{:S(2)}) collective-permute-start(f32[2,12,128,128]{3,2,1,0:T(8,128)S(1)} %collective-permute-done.30.refs_10_), channel_id=1, source_target_pairs={{0,1},{1,0},{2,3},{3,2},{4,5},{5,4},{6,7},{7,6},{8,9},{9,8},{10,11... | collective-permute-start | bytes 4718600 | tf_op jit(solution)/shard_map/ppermute | solution.py:30
  400.8 22.3 %collective-permute-start.33 = (f32[2,12,128,128]{3,2,1,0:T(8,128)}, f32[2,12,128,128]{3,2,1,0:T(8,128)}, u32[]{:S(2)}, u32[]{:S(2)}) collective-permute-start(f32[2,12,128,128]{3,2,1,0:T(8,128)} %collective-permute-done.31.refs_11_), channel_id=1, source_target_pairs={{0,1},{1,0},{2,3},{3,2},{4,5},{5,4},{6,7},{7,6},{8,9},{9,8},{10,11... | collective-permute-start | bytes 4718600 | tf_op jit(solution)/shard_map/ppermute | solution.py:30
  400.9 22.2 %collective-permute-start.36 = (f32[2,12,128,128]{3,2,1,0:T(8,128)}, f32[2,12,128,128]{3,2,1,0:T(8,128)}, u32[]{:S(2)}, u32[]{:S(2)}) collective-permute-start(f32[2,12,128,128]{3,2,1,0:T(8,128)} %collective-permute-done.34.refs_14_), channel_id=1, source_target_pairs={{0,1},{1,0},{2,3},{3,2},{4,5},{5,4},{6,7},{7,6},{8,9},{9,8},{10,11... | collective-permute-start | bytes 4718600 | tf_op jit(solution)/shard_map/ppermute | solution.py:30
  401.4 21.7 %collective-permute-start.37 = (f32[2,12,128,128]{3,2,1,0:T(8,128)}, f32[2,12,128,128]{3,2,1,0:T(8,128)}, u32[]{:S(2)}, u32[]{:S(2)}) collective-permute-start(f32[2,12,128,128]{3,2,1,0:T(8,128)} %collective-permute-done.35.refs_15_), channel_id=1, source_target_pairs={{0,1},{1,0},{2,3},{3,2},{4,5},{5,4},{6,7},{7,6},{8,9},{9,8},{10,11... | collective-permute-start | bytes 4718600 | tf_op jit(solution)/shard_map/ppermute | solution.py:30
  402.7 20.4 %collective-permute-start.43 = (f32[2,12,128,128]{3,2,1,0:T(8,128)}, f32[2,12,128,128]{3,2,1,0:T(8,128)}, u32[]{:S(2)}, u32[]{:S(2)}) collective-permute-start(f32[2,12,128,128]{3,2,1,0:T(8,128)} %broadcast_select_fusion.refs_19_), channel_id=1, source_target_pairs={{0,1},{1,0},{2,3},{3,2},{4,5},{5,4},{6,7},{7,6},{8,9},{9,8},{10,11... | collective-permute-start | bytes 4718600 | tf_op jit(solution)/shard_map/ppermute | solution.py:30
  407.2 15.9 %collective-permute-start.42 = (f32[2,12,128,128]{3,2,1,0:T(8,128)}, f32[2,12,128,128]{3,2,1,0:T(8,128)}, u32[]{:S(2)}, u32[]{:S(2)}) collective-permute-start(f32[2,12,128,128]{3,2,1,0:T(8,128)} %broadcast_select_fusion.1.refs_18_), channel_id=1, source_target_pairs={{0,1},{1,0},{2,3},{3,2},{4,5},{5,4},{6,7},{7,6},{8,9},{9,8},{10,11... | collective-permute-start | bytes 4718600 | tf_op jit(solution)/shard_map/ppermute | solution.py:30
  (17 other events, 513.8 us)

commit v2 on v1

v2 whole, which is shorter than its diff:
```python
import jax
import jax.numpy as jnp
from jax import lax
from jax.experimental import pallas as pl
from jax.experimental.pallas import tpu as pltpu
from jax.sharding import PartitionSpec as P

MESH = pl.DeviceIdType.MESH
CHUNKS = 8
GROUP = 4
TOGETHER = 2
CODE = 1024


def swap(array):
    return lax.ppermute(array, "rep", [(0, 1), (1, 0)])


def fetch_halo(sent, sent_base, swapped, chunks, size, collective_id):
    block = sent.shape[-1]
    at_x, at_y, at_z, at_second, at_swap, at_way = 0, 1, 2, 3, 8, 9

    def kernel(sent_ref, swapped_ref, out_ref, send_sem, recv_sem):
        n = lax.axis_size("rows")
        r = lax.axis_index("rows")
        q = lax.axis_index("rep")
        px, py = r % 2, (r // 2) % 2
        to_x = r + 1 - 2 * px
        to_y = r + 2 - 4 * py
        to_z = (r + n + 4 - 8 * py) % n
        from_z = (r + n - 4 + 8 * py) % n
        outer = px == py
        barrier = pltpu.get_barrier_semaphore()
        for rows, rep in ((to_x, q), (to_y, q), (from_z, q), (r, 1 - q)):
            pl.semaphore_signal(barrier, inc=1, device_id=(rows, rep), device_id_type=MESH)
        pl.semaphore_wait(barrier, 4)

        def span(c):
            return pl.ds(c * size, size)

        def copy(src, kind, place, c, target):
            return pltpu.make_async_remote_copy(
                src_ref=src,
                dst_ref=out_ref.at[place, span(c)],
                send_sem=send_sem.at[kind, c],
                recv_sem=recv_sem.at[place, c],
                device_id=target,
                device_id_type=MESH,
            )

        def own(c):
            return sent_ref.at[pl.ds(sent_base(q) + c * size, size)]

        def over_x(c):
            return copy(own(c), 0, at_x, c, (to_x, q))

        def over_y(c):
            return copy(own(c), 1, at_y, c, (to_y, q))

        def over_z(c):
            return copy(out_ref.at[at_y, span(c)], 2, at_z, c, (to_z, q))

        def second_x(c, held):
            return copy(out_ref.at[held, span(c)], 3, at_second, c, (to_x, q))

        def second_y(c):
            place = jnp.where(outer, at_second, at_way)
            return copy(out_ref.at[at_x, span(c)], 3, place, c, (to_y, q))

        def second_z(c):
            return copy(out_ref.at[at_way, span(c)], 9, at_second, c, (to_z, q))

        def share(place, c):
            return copy(out_ref.at[place, span(c)], 4 + place, 4 + place, c, (r, 1 - q))

        def own_share(c):
            return copy(swapped_ref.at[span(c)], 8, at_swap, c, (r, 1 - q))

        def arrived(place, c):
            copy(out_ref.at[place, span(c)], 0, place, c, (r, 1 - q)).wait_recv()

        pairs = [(c, c + 1) for c in range(0, chunks, 2)]
        x_order = [b for a, b in pairs] + [a for a, b in pairs]
        y_order = [a for a, b in pairs] + [b for a, b in pairs]
        ahead = 2
        for i in range(ahead):
            over_x(x_order[i]).start()
            over_y(y_order[i]).start()
        for i in range(chunks):
            c = x_order[i]
            arrived(at_x, c)
            if c % 2:
                second_y(c).start()
            if i + ahead < chunks:
                over_x(x_order[i + ahead]).start()
            share(at_x, c).start()
            own_share(i).start()
            c = y_order[i]
            arrived(at_y, c)
            over_z(c).start()
            if c % 2 == 0:

                @pl.when(outer)
                def _(c=c):
                    second_x(c, at_y).start()

            if i + ahead < chunks:
                over_y(y_order[i + ahead]).start()
            share(at_y, c).start()
            if i >= 1:
                c = y_order[i - 1]
                arrived(at_z, c)
                if c % 2 == 0:

                    @pl.when(jnp.logical_not(outer))
                    def _(c=c):
                        second_x(c, at_z).start()

                share(at_z, c).start()
            if 1 <= i <= len(pairs):
                c = x_order[i - 1]

                @pl.when(outer)
                def _(c=c):
                    arrived(at_way, c)
                    second_z(c).start()

            if i >= len(pairs):
                for c in pairs[i - len(pairs)]:
                    arrived(at_second, c)
                    share(at_second, c).start()
        c = y_order[-1]
        arrived(at_z, c)
        share(at_z, c).start()
        for c in range(chunks):
            for place in (4, 5, 6, 7, at_swap):
                arrived(place, c)
        for c in range(chunks):
            over_x(c).wait_send()
            over_y(c).wait_send()
            over_z(c).wait_send()
            second_x(c, at_z).wait_send()
            if c % 2:

                @pl.when(outer)
                def _(c=c):
                    second_z(c).wait_send()

            for place in (at_x, at_y, at_z, at_second):
                share(place, c).wait_send()
            own_share(c).wait_send()

    return pl.pallas_call(
        kernel,
        out_shape=jax.ShapeDtypeStruct((10, chunks * size, block, block), jnp.float32),
        in_specs=[pl.BlockSpec(memory_space=pl.ANY)] * 2,
        out_specs=pl.BlockSpec(memory_space=pl.ANY),
        scratch_shapes=[
            pltpu.SemaphoreType.DMA((10, chunks)),
            pltpu.SemaphoreType.DMA((10, chunks)),
        ],
        compiler_params=pltpu.CompilerParams(collective_id=collective_id, has_side_effects=True),
    )(sent, swapped)


def block_products(table, groups, sources, moves, lhs_moves, rows, slots, pool_blocks, entries, outs):
    block = sources[0].shape[-1]
    source_count = len(sources)
    transposed = entries is not None
    scalars = [groups, table] + ([entries] if transposed else [])
    scalar_count = len(scalars)

    def kernel(*refs):
        groups_ref, table_ref = refs[:2]
        source_refs = refs[scalar_count : scalar_count + source_count]
        out_ref, pool, lhs, high, low, sems, lhs_sems = refs[scalar_count + source_count :]

        def moved(index, move, target, semaphores):
            source, at, dst, count = move
            return pltpu.make_async_copy(
                source_refs[source].at[at], target.at[pl.ds(dst, count)], semaphores.at[index]
            )

        lhs_copies = [moved(i, move, lhs, lhs_sems) for i, move in enumerate(lhs_moves)]
        copies = [moved(i, move, pool, sems) for i, move in enumerate(moves)]
        for copy in lhs_copies:
            copy.start()
        if transposed:
            first, second = source_refs[-2:]
            bound = first.shape[0]

            def fetch(i, carry):
                code = refs[2][i]

                @pl.when(code < bound)
                def _():
                    pltpu.make_async_copy(first.at[code], lhs.at[i], lhs_sems.at[i]).start()

                @pl.when(code >= bound)
                def _():
                    pltpu.make_async_copy(
                        second.at[code - bound], lhs.at[i], lhs_sems.at[i]
                    ).start()

                return carry

            lax.fori_loop(0, rows * slots, fetch, 0)
        for copy in copies:
            copy.start()
        pool[pool_blocks] = jnp.zeros((block, block), jnp.float32)
        for copy in lhs_copies:
            copy.wait()

        def split(index, carry):
            for e in range(4):
                i = index * 4 + e
                if transposed:
                    pltpu.make_async_copy(source_refs[-2].at[0], lhs.at[i], lhs_sems.at[i]).wait()
                value = lhs[i].T if transposed else lhs[i]
                top = value.astype(jnp.bfloat16)
                high[i] = top
                low[i] = (value - top.astype(jnp.float32)).astype(jnp.bfloat16)
            return carry

        lax.fori_loop(0, rows * slots // 4, split, 0)
        for copy in copies:
            copy.wait()

        def term(o, g):
            row = o // outs
            left, right = [], []
            for e in range(GROUP):
                code = table_ref[o * slots + g * GROUP + e]
                s = row * slots + code // CODE
                value = pool[code % CODE]
                top = value.astype(jnp.bfloat16)
                rest = (value - top.astype(jnp.float32)).astype(jnp.bfloat16)
                left += [high[s], high[s], low[s]]
                right += [top, rest, top]
            return jnp.dot(
                jnp.concatenate(left, axis=1),
                jnp.concatenate(right, axis=0),
                preferred_element_type=jnp.float32,
            )

        def some_outputs(index, carry):
            first = index * TOGETHER
            steps = groups_ref[first]
            for e in range(1, TOGETHER):
                steps = jnp.maximum(steps, groups_ref[first + e])

            def one_group(g, totals):
                return tuple(totals[e] + term(first + e, g) for e in range(TOGETHER))

            zero = jnp.zeros((block, block), jnp.float32)
            totals = lax.fori_loop(0, steps, one_group, (zero,) * TOGETHER)
            for e in range(TOGETHER):
                out_ref[first + e] = totals[e]
            return carry

        lax.fori_loop(0, rows * outs // TOGETHER, some_outputs, 0)

    in_specs = (
        [pl.BlockSpec(memory_space=pltpu.SMEM)] * scalar_count
        + [pl.BlockSpec(memory_space=pl.ANY)] * source_count
    )
    result = pl.pallas_call(
        kernel,
        out_shape=jax.ShapeDtypeStruct((rows * outs, block, block), jnp.float32),
        in_specs=in_specs,
        out_specs=pl.BlockSpec(memory_space=pltpu.VMEM),
        scratch_shapes=[
            pltpu.VMEM((pool_blocks + 1, block, block), jnp.float32),
            pltpu.VMEM((rows * slots, block, block), jnp.float32),
            pltpu.VMEM((rows * slots, block, block), jnp.bfloat16),
            pltpu.VMEM((rows * slots, block, block), jnp.bfloat16),
            pltpu.SemaphoreType.DMA((len(moves),)),
            pltpu.SemaphoreType.DMA((rows * slots,)),
        ],
        compiler_params=pltpu.CompilerParams(vmem_limit_bytes=52 * 1024 * 1024),
        cost_estimate=pl.CostEstimate(
            flops=rows * outs * 10 * 6 * block**3 * 4,
            bytes_accessed=(pool_blocks + rows * (slots + outs)) * block * block * 4,
            transcendentals=0,
        ),
    )(*[scalar.reshape(-1) for scalar in scalars], *sources)
    return result.reshape(rows, outs, block, block)


def packed_list(found, codes, dummy):
    slots = found.shape[-1]
    index = jnp.arange(slots, dtype=jnp.int32)
    before = (index[:, None] > index[None, :]).astype(jnp.int32)
    rank = jnp.sum(found[..., None, :] * before, axis=-1)
    count = jnp.sum(found, axis=-1)
    chosen = found[..., None, :] * (rank[..., None, :] == index[:, None]).astype(jnp.int32)
    listed = jnp.sum(chosen * codes[..., None, :], axis=-1)
    listed = jnp.where(index < count[..., None], listed, dummy)
    return listed, (count + GROUP - 1) // GROUP


def shards(margin_blocks, margin_cols, factor_blocks, factor_cols, product_cols, metric_cols):
    rows, slots, block = factor_blocks.shape[:3]
    kept, kept_x = product_cols.shape[1], metric_cols.shape[1]
    half_rows, half_kept, half_x = rows // 2, kept // 2, kept_x // 2
    n = lax.axis_size("rows")
    r = lax.axis_index("rows")
    q = lax.axis_index("rep")
    place = r % 4
    int32 = jnp.int32

    sign_x = 1 - 2 * (place % 2)
    sign_y = 2 - 4 * (place // 2)
    patterns = jnp.concatenate([factor_cols, product_cols], axis=1)
    by_offset = [
        lax.ppermute(patterns, "rows", [(s, (s - o) % n) for s in range(n)]) if o else patterns
        for o in (-2, -1, 0, 1, 2)
    ]
    offsets = jnp.stack([0 * sign_x, sign_x, sign_y, -sign_y, -sign_x]).astype(int32)
    which = (offsets[:, None] == jnp.arange(-2, 3, dtype=int32)[None, :]).astype(int32)
    near_patterns = jnp.sum(which[:, :, None, None] * jnp.stack(by_offset)[None], axis=1)
    near_patterns = near_patterns.reshape(5 * rows, slots + kept)
    near_factor_cols = near_patterns[:, :slots]
    near_product_cols = near_patterns[:, slots:]
    near_index = jnp.arange(5 * rows, dtype=int32)
    row_of, slot_of = near_index % rows, near_index // rows
    swapped = slot_of * rows + ((row_of // half_rows) ^ q) * half_rows + row_of % half_rows
    factor_at = jnp.where(slot_of == 0, near_index, swapped).astype(int32)

    columns = jnp.concatenate([margin_cols, swap(margin_cols)], axis=1)
    offset = (columns // rows - r + 2) % n - 2
    slot = jnp.sum((offset[..., None] == offsets) * jnp.arange(5, dtype=int32), axis=-1)
    picked = (slot * rows + columns % rows)[..., None] == near_index
    picked = picked.astype(int32)
    picked_cols = jnp.sum(picked[..., None] * near_factor_cols, axis=2)
    picked_at = jnp.sum(picked * factor_at, axis=2)
    my_product_cols = lax.dynamic_slice_in_dim(product_cols, q * half_kept, half_kept, 1)
    match = (picked_cols[:, None] == my_product_cols[:, :, None, None]).astype(int32)
    m_index = jnp.arange(slots, dtype=int32)
    k_index = jnp.arange(columns.shape[1], dtype=int32)
    code = k_index[:, None] * CODE + picked_at[:, None, :, None] * slots + m_index
    table, groups = packed_list(
        jnp.sum(match, axis=-1), jnp.sum(match * code, axis=-1), 5 * rows * slots
    )

    table, groups, factor_blocks, margin_blocks = lax.optimization_barrier(
        (table, groups, factor_blocks, margin_blocks)
    )
    share = half_rows * slots
    flat_factor = factor_blocks.reshape(-1, block, block)
    flat_margin = margin_blocks.reshape(-1, block, block)
    near = fetch_halo(flat_factor, lambda core: core * share, flat_margin, CHUNKS, share // CHUNKS, 0)
    moves = [(0, slice(None), 0, rows * slots)]
    for j in range(4):
        for h in range(2):
            moves.append((1, j + 4 * h, ((j + 1) * rows + h * half_rows) * slots, share))
    mine = margin_blocks.shape[1]
    lhs_moves = []
    for row in range(rows):
        lhs_moves.append((2, pl.ds(row * mine, mine), row * slots, mine))
        lhs_moves.append((1, (8, pl.ds(row * mine, mine)), row * slots + mine, mine))
    product = block_products(
        table,
        groups,
        [flat_factor, near, flat_margin],
        moves,
        lhs_moves,
        rows,
        slots,
        5 * rows * slots,
        None,
        half_kept,
    )

    targets = r * rows + jnp.arange(rows, dtype=int32)
    hit = (near_factor_cols[None] == targets[:, None, None]).astype(int32)
    held = jnp.sum(hit, axis=-1)
    near_at = rows + (slot_of - 1 + 4 * ((row_of // half_rows) ^ q)) * half_rows + row_of % half_rows
    near_at = jnp.where(slot_of == 0, near_index, near_at)
    at = jnp.sum(hit * (near_at[:, None] * slots + m_index), axis=-1)
    entry_span = 9 * rows * slots
    entry_code, _ = packed_list(held, near_index * entry_span + at, 0)
    entry_code = entry_code[:, :slots]
    entry_row, entry_at = entry_code // entry_span, entry_code % entry_span
    order = jnp.where(q == 0, near_product_cols, jnp.roll(near_product_cols, half_kept, axis=1))
    entry_pick = (entry_row[..., None] == near_index).astype(int32)
    entry_cols = jnp.sum(entry_pick[..., None] * order, axis=2)
    my_metric_cols = lax.dynamic_slice_in_dim(metric_cols, q * half_x, half_x, 1)
    match = (entry_cols[:, None] == my_metric_cols[:, :, None, None]).astype(int32)
    y_index = jnp.arange(kept, dtype=int32)
    entry_base = (entry_row // rows) * rows * kept + entry_row % rows * half_kept
    y_at = y_index // half_kept * (rows * half_kept) + y_index % half_kept
    code = m_index[:, None] * CODE + entry_base[:, None, :, None] + y_at
    table, groups = packed_list(
        jnp.sum(match, axis=-1), jnp.sum(match * code, axis=-1), 5 * rows * kept
    )

    share = rows * half_kept
    flat_product = product.reshape(-1, block, block)
    near_product = fetch_halo(
        flat_product, lambda core: 0, flat_product, CHUNKS, share // CHUNKS, 1
    )
    moves = [(0, slice(None), 0, share), (1, 8, share, share)]
    for j in range(4):
        for h in range(2):
            moves.append((1, j + 4 * h, (2 * j + 2 + h) * share, share))
    metric = block_products(
        table,
        groups,
        [flat_product, near_product, flat_factor, near.reshape(-1, block, block)],
        moves,
        [],
        rows,
        slots,
        5 * rows * kept,
        entry_at,
        half_x,
    )
    return (product, metric)


def solution(mesh):
    return jax.shard_map(
        shards,
        mesh=mesh,
        in_specs=(
            P("rows", "rep", None, None),
            P("rows", "rep"),
            P("rows", None, None, None),
            P("rows", None),
            P("rows", None),
            P("rows", None),
        ),
        out_specs=(P("rows", "rep", None, None), P("rows", "rep", None, None)),
        check_vma=False,
    )
```

time: 479 us -> 312 us (0.65); the launches traced: 474 us -> 312 us
  waiting for transfers between devices: 252 us -> 0.2 us
  Pallas kernels: 89 us -> 285 us
  starting transfers between devices: 70 us -> 9.02 us
  local copies, waits for them, and re-layouts: 42.1 us -> 1.71 us
  other arithmetic: 19.5 us -> 14.6 us
    pallas_call x0 -> x2, Pallas kernels: none -> 208 us  [fetch_halo(): pl.pallas_call(kernel, out_shape=jax.ShapeDtypeStruct((10, chunks * size,...]
    ppermute x20 -> x0, waiting for transfers between devices: 206 us -> none  [hop(): lax.ppermute(array, 'rows', [(s, target(s, n)) for s in range(n) if s % 4...]
    ppermute x4, waiting for transfers between devices: 39.8 us -> 0.2 us  [shards(): lax.ppermute(patterns, 'rows', [(s, (s - o) % n) for s in range(n)])]
    ppermute x20 -> x1, starting transfers between devices: 35.8 us -> 1.52 us  [swap(): return lax.ppermute(array, 'rep', [(0, 1), (1, 0)])]
    ppermute x20 -> x0, starting transfers between devices: 28.2 us -> none  [hop(): lax.ppermute(array, 'rows', [(s, target(s, n)) for s in range(n) if s % 4...]
    unnamed x60 -> x6, local copies, waits for them, and re-layouts: 24.6 us -> 0.03 us
    pallas_call x2, Pallas kernels: 89 us -> 77.5 us  [block_products(): pl.pallas_call(kernel, out_shape=jax.ShapeDtypeStruct((rows * outs, block...]
    gather x1 -> x0, local copies, waits for them, and re-layouts: 9.76 us -> none  [shards(): entries = flat[entry_at]]
  transfers between devices with their start and end apart: 44 -> 5, of which waited for: 18 -> 1; matrix products, arithmetic and copies ran while one was open for 12% -> 1% of each run, Pallas kernels for 0% -> 0%
where the time goes in v2:
time: 312 us
  Pallas kernels  285 us (91%)
  other arithmetic  14.6 us (5%)
  starting transfers between devices  9.02 us (3%)
    pallas_call x2, Pallas kernels, fetch_halo(): pl.pallas_call(kernel, out_shape=jax.ShapeDtypeStruct((10, chunks * size,...  208 us
    pallas_call x2, Pallas kernels, block_products(): pl.pallas_call(kernel, out_shape=jax.ShapeDtypeStruct((rows * outs, block...  77.5 us
    ppermute x4, starting transfers between devices, shards(): lax.ppermute(patterns, 'rows', [(s, (s - o) % n) for s in range(n)])  7.5 us
  transfers between devices with their start and end apart: 5, of which 1 were waited for; matrix products, arithmetic and copies ran while one was open for 1% of the time, Pallas kernels for 0%

profile of v2, /device:TPU:1, one launch (start us, length us, event | category | flops | bytes accessed | tf_op | source)
XLA Modules:
  0.0 311.7 jit_solution(252610399054592320)
XLA Ops:
  0.6 0.0 copy-start
  0.6 0.8 pad_add_fusion.1
  1.4 5.1 %collective-permute-start.4 = (s32[4,40]{1,0:T(4,128)S(1)}, s32[4,40]{1,0:T(4,128)S(1)}, u32[]{:S(2)}, u32[]{:S(2)}) collective-permute-start(s32[4,40]{1,0:T(4,128)S(1)} %pad_add_fusion.1), channel_id=1, source_target_pairs={{0,28},{2,30},{4,0},{6,2},{8,4},{10,6},{12,8},{14,10},{16,12},{18,... | collective-permute-start | bytes 1928 | tf_op jit(solution)/shard_map/ppermute | solution.py:316
  6.5 1.2 collective-permute-start.3
  7.7 0.3 collective-permute-start.2
  8.0 0.9 collective-permute-start.1
  8.9 1.5 collective-permute-start
  10.6 0.8 constant_dynamic-slice_fusion.1
  11.3 0.1 constant_dynamic-slice_fusion
  11.4 0.1 stack.37
  11.5 0.1 compare_convert_fusion
  11.6 0.8 fusion.12
  12.4 0.1 select_reduce_fusion.1
  12.4 0.8 fusion.13
  13.2 0.1 fusion.4
  13.3 0.2 select_reduce_fusion
  13.5 0.0 collective-permute-done.1
  13.5 0.2 collective-permute-done.2
  13.7 0.0 collective-permute-done.3
  13.8 0.1 multiply_reduce_fusion.6
  13.9 0.1 fusion.29
  14.0 0.1 copy.8
  14.0 0.2 convert_reduce_fusion.5
  14.3 0.4 multiply_reduce_fusion.8
  14.7 0.1 copy.10
  14.8 0.4 multiply_reduce_fusion.7
  15.2 0.1 copy.11
  15.3 0.1 fusion.21
  15.4 0.1 reshape.481.refs_2_
  15.5 1.2 multiply_reduce_fusion.1
  16.7 0.1 iota_add_fusion
  16.7 2.6 convert_reduce_fusion.3
  19.4 0.1 broadcast_add_fusion
  19.5 0.1 slice_select_fusion
  19.5 0.2 multiply_reduce_fusion
  19.8 2.6 convert_reduce_fusion
  22.4 0.1 sub.95
  22.5 1.7 multiply_reduce_fusion.3
  24.2 1.7 multiply_reduce_fusion.2
  25.9 0.1 fusion.6
  26.0 0.1 select_n.215.refs_1_
  26.1 0.1 fusion.5
  26.2 0.1 reshape.476.refs_0_
  26.3 0.1 reshape.477.refs_1_
  26.3 85.2 %shard_map.77.refs_3_ = f32[10,32,128,128]{3,2,1,0:T(8,128)} custom-call(f32[64,128,128]{2,1,0:T(8,128)} %bitcast.22, f32[32,128,128]{2,1,0:T(8,128)} %bitcast.25), custom_call_target="tpu_custom_call" | custom-call | tf_op jit(solution)/shard_map/pallas_call | solution.py:153
  111.6 34.2 %shard_map.78.sent_ref.swapped_ref.refs_3_ = f32[48,128,128]{2,1,0:T(8,128)} custom-call(s32[48]{0:T(128)S(1)} %reshape.476.refs_0_, s32[768]{0:T(1024)S(1)} %reshape.477.refs_1_, f32[64,128,128]{2,1,0:T(8,128)} %bitcast.23, f32[10,32,128,128]{3,2,1,0:T(8,128)} %shard_map.77.refs_3_, f32[32,128,128]{2,1,0:T(8,128)} %bitcast.26), custom_call_target="tpu_custom_call" | custom-call | flops 24159191040 | bytes 28311552 | tf_op jit(solution)/shard_map/pallas_call | solution.py:267
  145.8 122.7 %shard_map.79.refs_4_ = f32[10,48,128,128]{3,2,1,0:T(8,128)} custom-call(f32[48,128,128]{2,1,0:T(8,128)} %shard_map.78.sent_ref.swapped_ref.refs_3_, f32[48,128,128]{2,1,0:T(8,128)} %shard_map.78.sent_ref.swapped_ref.refs_3_), custom_call_target="tpu_custom_call" | custom-call | tf_op jit(solution)/shard_map/pallas_call | solution.py:153
  268.4 43.3 %shard_map.80 = f32[48,128,128]{2,1,0:T(8,128)} custom-call(s32[48]{0:T(128)S(1)} %and_select_fusion.2.refs_0_, s32[768]{0:T(1024)S(1)} %select_n.215.refs_1_, s32[64]{0:T(128)S(1)} %reshape.481.refs_2_, f32[48,128,128]{2,1,0:T(8,128)} %shard_map.78.sent_ref.swapped_ref.refs_3_, f32[10,48,128,128]{3,2,1,0:T(8,128)} %shard_map.79.refs_4_, ...), custom_call_target="tpu_custom_call" | custom-call | flops 24159191040 | bytes 38797312 | tf_op jit(solution)/shard_map/pallas_call | solution.py:267
  (25 shorter events, 0.2 us)
Async XLA Ops:
  0.6 10.7 %copy-start = (s32[4,24]{1,0:T(4,128)S(1)}, s32[4,24]{1,0:T(4,128)}, u32[]{:S(2)}) copy-start(s32[4,24]{1,0:T(4,128)} %param.11) | copy-start | bytes 1156
  1.4 12.3 %collective-permute-start.4 = (s32[4,40]{1,0:T(4,128)S(1)}, s32[4,40]{1,0:T(4,128)S(1)}, u32[]{:S(2)}, u32[]{:S(2)}) collective-permute-start(s32[4,40]{1,0:T(4,128)S(1)} %pad_add_fusion.1), channel_id=1, source_target_pairs={{0,28},{2,30},{4,0},{6,2},{8,4},{10,6},{12,8},{14,10},{16,12},{18,... | collective-permute-start | bytes 1928 | tf_op jit(solution)/shard_map/ppermute | solution.py:316
  6.5 7.2 %collective-permute-start.3 = (s32[4,40]{1,0:T(4,128)S(1)}, s32[4,40]{1,0:T(4,128)S(1)}, u32[]{:S(2)}, u32[]{:S(2)}) collective-permute-start(s32[4,40]{1,0:T(4,128)S(1)} %pad_add_fusion.1), channel_id=1, source_target_pairs={{0,30},{2,0},{4,2},{6,4},{8,6},{10,8},{12,10},{14,12},{16,14},{18,... | collective-permute-start | bytes 1928 | tf_op jit(solution)/shard_map/ppermute | solution.py:316
  7.7 6.0 %collective-permute-start.2 = (s32[4,40]{1,0:T(4,128)S(1)}, s32[4,40]{1,0:T(4,128)S(1)}, u32[]{:S(2)}, u32[]{:S(2)}) collective-permute-start(s32[4,40]{1,0:T(4,128)S(1)} %pad_add_fusion.1), channel_id=1, source_target_pairs={{0,2},{2,4},{4,6},{6,8},{8,10},{10,12},{12,14},{14,16},{16,18},{18... | collective-permute-start | bytes 1928 | tf_op jit(solution)/shard_map/ppermute | solution.py:316
  8.0 5.5 %collective-permute-start.1 = (s32[4,40]{1,0:T(4,128)S(1)}, s32[4,40]{1,0:T(4,128)S(1)}, u32[]{:S(2)}, u32[]{:S(2)}) collective-permute-start(s32[4,40]{1,0:T(4,128)S(1)} %pad_add_fusion.1), channel_id=1, source_target_pairs={{0,4},{2,6},{4,8},{6,10},{8,12},{10,14},{12,16},{14,18},{16,20},{1... | collective-permute-start | bytes 1928 | tf_op jit(solution)/shard_map/ppermute | solution.py:316
  8.9 2.7 collective-permute-start

commit v3 on v2

--- a/solution.py
+++ b/solution.py
@@ -12,15 +12,15 @@
 CODE = 1024
 
 
-def swap(array):
-    return lax.ppermute(array, "rep", [(0, 1), (1, 0)])
-
-
-def fetch_halo(sent, sent_base, swapped, chunks, size, collective_id):
+def fetch_halo(sent, sent_base, swapped, chunks, size, collective_id, tile=None):
     block = sent.shape[-1]
     at_x, at_y, at_z, at_second, at_swap, at_way = 0, 1, 2, 3, 8, 9
 
-    def kernel(sent_ref, swapped_ref, out_ref, send_sem, recv_sem):
+    def kernel(*refs):
+        if tile is None:
+            sent_ref, swapped_ref, out_ref, send_sem, recv_sem = refs
+        else:
+            sent_ref, swapped_ref, tile_ref, out_ref, tiles_ref, send_sem, recv_sem, tile_sem = refs
         n = lax.axis_size("rows")
         r = lax.axis_index("rows")
         q = lax.axis_index("rep")
@@ -79,6 +79,29 @@
         def arrived(place, c):
             copy(out_ref.at[place, span(c)], 0, place, c, (r, 1 - q)).wait_recv()
 
+        def tile_copy(src, kind, place, target):
+            return pltpu.make_async_remote_copy(
+                src_ref=src,
+                dst_ref=tiles_ref.at[place],
+                send_sem=tile_sem.at[0, kind],
+                recv_sem=tile_sem.at[1, place],
+                device_id=target,
+                device_id_type=MESH,
+            )
+
+        tile_hops = []
+        if tile is not None:
+            tile_hops = [
+                tile_copy(tile_ref, 1, 1, (to_x, q)),
+                tile_copy(tile_ref, 2, 2, (to_y, q)),
+                tile_copy(tile_ref, 5, 5, (r, 1 - q)),
+                tile_copy(tiles_ref.at[2], 3, 3, (to_z, q)),
+            ]
+            own_tile = pltpu.make_async_copy(tile_ref, tiles_ref.at[0], tile_sem.at[0, 0])
+            own_tile.start()
+            for tile_hop in tile_hops[:3]:
+                tile_hop.start()
+
         pairs = [(c, c + 1) for c in range(0, chunks, 2)]
         x_order = [b for a, b in pairs] + [a for a, b in pairs]
         y_order = [a for a, b in pairs] + [b for a, b in pairs]
@@ -86,6 +109,9 @@
         for i in range(ahead):
             over_x(x_order[i]).start()
             over_y(y_order[i]).start()
+        if tile is not None:
+            tile_hops[1].wait_recv()
+            tile_hops[3].start()
         for i in range(chunks):
             c = x_order[i]
             arrived(at_x, c)
@@ -129,6 +155,24 @@
                 for c in pairs[i - len(pairs)]:
                     arrived(at_second, c)
                     share(at_second, c).start()
+        if tile is not None:
+            tile_hops[3].wait_recv()
+
+            @pl.when(outer)
+            def _():
+                tile_copy(tiles_ref.at[2], 4, 4, (to_x, q)).start()
+
+            @pl.when(jnp.logical_not(outer))
+            def _():
+                tile_copy(tiles_ref.at[3], 4, 4, (to_x, q)).start()
+
+            tile_hops.append(tile_copy(tiles_ref.at[2], 4, 4, (to_x, q)))
+            tile_hops[4].wait_recv()
+            tile_hops[0].wait_recv()
+            tile_hops[2].wait_recv()
+            own_tile.wait()
+            for tile_hop in tile_hops:
+                tile_hop.wait_send()
         c = y_order[-1]
         arrived(at_z, c)
         share(at_z, c).start()
@@ -150,30 +194,33 @@
                 share(place, c).wait_send()
             own_share(c).wait_send()
 
+    anywhere = pl.BlockSpec(memory_space=pl.ANY)
+    out_shape = [jax.ShapeDtypeStruct((10, chunks * size, block, block), jnp.float32)]
+    scratch = [pltpu.SemaphoreType.DMA((10, chunks)), pltpu.SemaphoreType.DMA((10, chunks))]
+    operands = [sent, swapped]
+    if tile is not None:
+        out_shape.append(jax.ShapeDtypeStruct((6,) + tile.shape, tile.dtype))
+        scratch.append(pltpu.SemaphoreType.DMA((2, 6)))
+        operands.append(tile)
     return pl.pallas_call(
         kernel,
-        out_shape=jax.ShapeDtypeStruct((10, chunks * size, block, block), jnp.float32),
-        in_specs=[pl.BlockSpec(memory_space=pl.ANY)] * 2,
-        out_specs=pl.BlockSpec(memory_space=pl.ANY),
-        scratch_shapes=[
-            pltpu.SemaphoreType.DMA((10, chunks)),
-            pltpu.SemaphoreType.DMA((10, chunks)),
-        ],
+        out_shape=out_shape,
+        in_specs=[anywhere] * len(operands),
+        out_specs=[anywhere] * len(out_shape),
+        scratch_shapes=scratch,
         compiler_params=pltpu.CompilerParams(collective_id=collective_id, has_side_effects=True),
-    )(sent, swapped)
-
-
-def block_products(table, groups, sources, moves, lhs_moves, rows, slots, pool_blocks, entries, outs):
+    )(*operands)
+
+
+def block_products(tiles, build, sources, moves, lhs_moves, rows, slots, pool_blocks, transposed, outs, n):
     block = sources[0].shape[-1]
     source_count = len(sources)
-    transposed = entries is not None
-    scalars = [groups, table] + ([entries] if transposed else [])
-    scalar_count = len(scalars)
 
     def kernel(*refs):
-        groups_ref, table_ref = refs[:2]
-        source_refs = refs[scalar_count : scalar_count + source_count]
-        out_ref, pool, lhs, high, low, sems, lhs_sems = refs[scalar_count + source_count :]
+        tiles_ref = refs[0]
+        source_refs = refs[1 : 1 + source_count]
+        out_ref, pool, lhs, high, low, sems, lhs_sems = refs[1 + source_count : 8 + source_count]
+        table_ref, count_ref, where_ref, entry_ref = refs[8 + source_count :]
 
         def moved(index, move, target, semaphores):
             source, at, dst, count = move
@@ -183,14 +230,16 @@
 
         lhs_copies = [moved(i, move, lhs, lhs_sems) for i, move in enumerate(lhs_moves)]
         copies = [moved(i, move, pool, sems) for i, move in enumerate(moves)]
-        for copy in lhs_copies:
+        for copy in lhs_copies + copies:
             copy.start()
+        build_entries, build_pairs = build
         if transposed:
+            build_entries(tiles_ref, entry_ref, count_ref)
             first, second = source_refs[-2:]
             bound = first.shape[0]
 
             def fetch(i, carry):
-                code = refs[2][i]
+                code = entry_ref[i // slots * 2 * slots + i % slots] // CODE
 
                 @pl.when(code < bound)
                 def _():
@@ -205,9 +254,29 @@
                 return carry
 
             lax.fori_loop(0, rows * slots, fetch, 0)
-        for copy in copies:
-            copy.start()
         pool[pool_blocks] = jnp.zeros((block, block), jnp.float32)
+
+        def clear(i, carry):
+            for e in range(slots):
+                table_ref[i * slots + e] = jnp.int32(pool_blocks)
+            return carry
+
+        lax.fori_loop(0, rows * outs, clear, 0)
+
+        def forget(i, carry):
+            for e in range(rows):
+                where_ref[i * rows + e] = jnp.int32(outs)
+            return carry
+
+        lax.fori_loop(0, n, forget, 0)
+        lax.fori_loop(
+            0,
+            rows,
+            lambda row, carry: build_pairs(
+                row, tiles_ref, table_ref, count_ref, where_ref, entry_ref
+            ),
+            0,
+        )
         for copy in lhs_copies:
             copy.wait()
 
@@ -245,9 +314,11 @@
 
         def some_outputs(index, carry):
             first = index * TOGETHER
-            steps = groups_ref[first]
+            counts = first // outs * (outs + 1) + first % outs
+            steps = count_ref[counts]
             for e in range(1, TOGETHER):
-                steps = jnp.maximum(steps, groups_ref[first + e])
+                steps = jnp.maximum(steps, count_ref[counts + e])
+            steps = (steps + GROUP - 1) // GROUP
 
             def one_group(g, totals):
                 return tuple(totals[e] + term(first + e, g) for e in range(TOGETHER))
@@ -261,7 +332,7 @@
         lax.fori_loop(0, rows * outs // TOGETHER, some_outputs, 0)
 
     in_specs = (
-        [pl.BlockSpec(memory_space=pltpu.SMEM)] * scalar_count
+        [pl.BlockSpec(memory_space=pltpu.SMEM)]
         + [pl.BlockSpec(memory_space=pl.ANY)] * source_count
     )
     result = pl.pallas_call(
@@ -276,6 +347,10 @@
             pltpu.VMEM((rows * slots, block, block), jnp.bfloat16),
             pltpu.SemaphoreType.DMA((len(moves),)),
             pltpu.SemaphoreType.DMA((rows * slots,)),
+            pltpu.SMEM((rows * outs * slots + 2048,), jnp.int32),
+            pltpu.SMEM((rows * (outs + 1) + 8,), jnp.int32),
+            pltpu.SMEM((n * rows,), jnp.int32),
+            pltpu.SMEM((rows * 2 * slots + 1024,), jnp.int32),
         ],
         compiler_params=pltpu.CompilerParams(vmem_limit_bytes=52 * 1024 * 1024),
         cost_estimate=pl.CostEstimate(
@@ -283,20 +358,8 @@
             bytes_accessed=(pool_blocks + rows * (slots + outs)) * block * block * 4,
             transcendentals=0,
         ),
-    )(*[scalar.reshape(-1) for scalar in scalars], *sources)
+    )(tiles, *sources)
     return result.reshape(rows, outs, block, block)
-
-
-def packed_list(found, codes, dummy):
-    slots = found.shape[-1]
-    index = jnp.arange(slots, dtype=jnp.int32)
-    before = (index[:, None] > index[None, :]).astype(jnp.int32)
-    rank = jnp.sum(found[..., None, :] * before, axis=-1)
-    count = jnp.sum(found, axis=-1)
-    chosen = found[..., None, :] * (rank[..., None, :] == index[:, None]).astype(jnp.int32)
-    listed = jnp.sum(chosen * codes[..., None, :], axis=-1)
-    listed = jnp.where(index < count[..., None], listed, dummy)
-    return listed, (count + GROUP - 1) // GROUP
 
 
 def shards(margin_blocks, margin_cols, factor_blocks, factor_cols, product_cols, metric_cols):
@@ -306,98 +369,126 @@
     n = lax.axis_size("rows")
     r = lax.axis_index("rows")
     q = lax.axis_index("rep")
-    place = r % 4
-    int32 = jnp.int32
-
-    sign_x = 1 - 2 * (place % 2)
-    sign_y = 2 - 4 * (place // 2)
-    patterns = jnp.concatenate([factor_cols, product_cols], axis=1)
-    by_offset = [
-        lax.ppermute(patterns, "rows", [(s, (s - o) % n) for s in range(n)]) if o else patterns
-        for o in (-2, -1, 0, 1, 2)
-    ]
-    offsets = jnp.stack([0 * sign_x, sign_x, sign_y, -sign_y, -sign_x]).astype(int32)
-    which = (offsets[:, None] == jnp.arange(-2, 3, dtype=int32)[None, :]).astype(int32)
-    near_patterns = jnp.sum(which[:, :, None, None] * jnp.stack(by_offset)[None], axis=1)
-    near_patterns = near_patterns.reshape(5 * rows, slots + kept)
-    near_factor_cols = near_patterns[:, :slots]
-    near_product_cols = near_patterns[:, slots:]
-    near_index = jnp.arange(5 * rows, dtype=int32)
-    row_of, slot_of = near_index % rows, near_index // rows
-    swapped = slot_of * rows + ((row_of // half_rows) ^ q) * half_rows + row_of % half_rows
-    factor_at = jnp.where(slot_of == 0, near_index, swapped).astype(int32)
-
-    columns = jnp.concatenate([margin_cols, swap(margin_cols)], axis=1)
-    offset = (columns // rows - r + 2) % n - 2
-    slot = jnp.sum((offset[..., None] == offsets) * jnp.arange(5, dtype=int32), axis=-1)
-    picked = (slot * rows + columns % rows)[..., None] == near_index
-    picked = picked.astype(int32)
-    picked_cols = jnp.sum(picked[..., None] * near_factor_cols, axis=2)
-    picked_at = jnp.sum(picked * factor_at, axis=2)
-    my_product_cols = lax.dynamic_slice_in_dim(product_cols, q * half_kept, half_kept, 1)
-    match = (picked_cols[:, None] == my_product_cols[:, :, None, None]).astype(int32)
-    m_index = jnp.arange(slots, dtype=int32)
-    k_index = jnp.arange(columns.shape[1], dtype=int32)
-    code = k_index[:, None] * CODE + picked_at[:, None, :, None] * slots + m_index
-    table, groups = packed_list(
-        jnp.sum(match, axis=-1), jnp.sum(match * code, axis=-1), 5 * rows * slots
-    )
-
-    table, groups, factor_blocks, margin_blocks = lax.optimization_barrier(
-        (table, groups, factor_blocks, margin_blocks)
-    )
+    mine = margin_blocks.shape[1]
+    at_kept, at_margin = slots, slots + kept
+    at_metric = at_margin + mine
+    at_place = at_metric + kept_x
+    ones = jnp.ones((rows, 1), jnp.int32)
+    tile = jnp.concatenate(
+        [factor_cols, product_cols, margin_cols, metric_cols, r * ones, q * ones], axis=1
+    )
+    tile = jnp.pad(tile, ((0, 8 - rows), (0, 128 - tile.shape[1])))
+
+    def place_of(tiles):
+        return tiles[0, 0, at_place], tiles[0, 0, at_place + 1]
+
+    def append(row, out, code, outs, table, counts):
+        count = counts[row * (outs + 1) + out]
+        start = jnp.where(out == outs, rows * outs, row * outs + out)
+        table[start * slots + count] = code
+        counts[row * (outs + 1) + out] = count + 1
+
+    def product_pairs(row, tiles, table, counts, where, entry):
+        mr, mq = place_of(tiles)
+        sign_x = 1 - 2 * (mr % 2)
+        sign_y = 2 - 4 * (mr // 2 % 2)
+        for y in range(half_kept):
+            where[tiles[0, row, at_kept + mq * half_kept + y]] = jnp.int32(y)
+        for y in range(half_kept + 1):
+            counts[row * (half_kept + 1) + y] = jnp.int32(0)
+
+        def one_margin(k, carry):
+            theirs = k // mine
+            column = tiles[5 * theirs, row, at_margin + k % mine]
+            offset = (column // rows - mr + 2 + n) % n - 2
+            slot = jnp.where(offset == sign_x, 1, jnp.where(offset == sign_y, 2, 3))
+            slot = jnp.where(offset == -sign_x, 4, jnp.where(offset == 0, 0, slot))
+            inner = column % rows
+            swapped = ((inner // half_rows) ^ mq) * half_rows + inner % half_rows
+            base = k * CODE + (slot * rows + jnp.where(slot == 0, inner, swapped)) * slots
+            for m in range(slots):
+                out = where[tiles[slot, inner, m]]
+                append(row, out, base + m, half_kept, table, counts)
+            return carry
+
+        lax.fori_loop(0, 2 * mine, one_margin, 0)
+        for y in range(half_kept):
+            where[tiles[0, row, at_kept + mq * half_kept + y]] = jnp.int32(half_kept)
+        return 0
+
+    def metric_entries(tiles, entry, counts):
+        mr, mq = place_of(tiles)
+        for a in range(rows + 1):
+            counts[a] = jnp.int32(0)
+
+        def one_row(near_row, carry):
+            slot, inner = near_row // rows, near_row % rows
+            other = (inner // half_rows) ^ mq
+            held = rows + (slot - 1 + 4 * other) * half_rows + inner % half_rows
+            base = jnp.where(slot == 0, inner, held) * slots
+            for m in range(slots):
+                a = tiles[slot, inner, m] - mr * rows
+                a = jnp.where((a >= 0) & (a < rows), a, rows)
+                count = counts[a]
+                entry[a * 2 * slots + count] = (base + m) * CODE + near_row
+                counts[a] = count + 1
+            return carry
+
+        lax.fori_loop(0, 5 * rows, one_row, 0)
+
+    def metric_pairs(row, tiles, table, counts, where, entry):
+        mr, mq = place_of(tiles)
+        for x in range(half_x):
+            where[tiles[0, row, at_metric + mq * half_x + x]] = jnp.int32(x)
+        for x in range(half_x + 1):
+            counts[row * (half_x + 1) + x] = jnp.int32(0)
+
+        def one_entry(t, carry):
+            near_row = entry[row * 2 * slots + t] % CODE
+            slot, inner = near_row // rows, near_row % rows
+            for h in range(2):
+                base = ((2 * slot + (h ^ mq)) * rows + inner) * half_kept + t * CODE
+                for y in range(half_kept):
+                    out = where[tiles[slot, inner, at_kept + h * half_kept + y]]
+                    append(row, out, base + y, half_x, table, counts)
+            return carry
+
+        lax.fori_loop(0, slots, one_entry, 0)
+        for x in range(half_x):
+            where[tiles[0, row, at_metric + mq * half_x + x]] = jnp.int32(half_x)
+        return 0
+
     share = half_rows * slots
     flat_factor = factor_blocks.reshape(-1, block, block)
     flat_margin = margin_blocks.reshape(-1, block, block)
-    near = fetch_halo(flat_factor, lambda core: core * share, flat_margin, CHUNKS, share // CHUNKS, 0)
+    near, tiles = fetch_halo(
+        flat_factor, lambda core: core * share, flat_margin, CHUNKS, share // CHUNKS, 0, tile
+    )
     moves = [(0, slice(None), 0, rows * slots)]
     for j in range(4):
         for h in range(2):
             moves.append((1, j + 4 * h, ((j + 1) * rows + h * half_rows) * slots, share))
-    mine = margin_blocks.shape[1]
     lhs_moves = []
     for row in range(rows):
         lhs_moves.append((2, pl.ds(row * mine, mine), row * slots, mine))
         lhs_moves.append((1, (8, pl.ds(row * mine, mine)), row * slots + mine, mine))
     product = block_products(
-        table,
-        groups,
+        tiles,
+        (None, product_pairs),
         [flat_factor, near, flat_margin],
         moves,
         lhs_moves,
         rows,
         slots,
         5 * rows * slots,
-        None,
+        False,
         half_kept,
-    )
-
-    targets = r * rows + jnp.arange(rows, dtype=int32)
-    hit = (near_factor_cols[None] == targets[:, None, None]).astype(int32)
-    held = jnp.sum(hit, axis=-1)
-    near_at = rows + (slot_of - 1 + 4 * ((row_of // half_rows) ^ q)) * half_rows + row_of % half_rows
-    near_at = jnp.where(slot_of == 0, near_index, near_at)
-    at = jnp.sum(hit * (near_at[:, None] * slots + m_index), axis=-1)
-    entry_span = 9 * rows * slots
-    entry_code, _ = packed_list(held, near_index * entry_span + at, 0)
-    entry_code = entry_code[:, :slots]
-    entry_row, entry_at = entry_code // entry_span, entry_code % entry_span
-    order = jnp.where(q == 0, near_product_cols, jnp.roll(near_product_cols, half_kept, axis=1))
-    entry_pick = (entry_row[..., None] == near_index).astype(int32)
-    entry_cols = jnp.sum(entry_pick[..., None] * order, axis=2)
-    my_metric_cols = lax.dynamic_slice_in_dim(metric_cols, q * half_x, half_x, 1)
-    match = (entry_cols[:, None] == my_metric_cols[:, :, None, None]).astype(int32)
-    y_index = jnp.arange(kept, dtype=int32)
-    entry_base = (entry_row // rows) * rows * kept + entry_row % rows * half_kept
-    y_at = y_index // half_kept * (rows * half_kept) + y_index % half_kept
-    code = m_index[:, None] * CODE + entry_base[:, None, :, None] + y_at
-    table, groups = packed_list(
-        jnp.sum(match, axis=-1), jnp.sum(match * code, axis=-1), 5 * rows * kept
+        n,
     )
 
     share = rows * half_kept
     flat_product = product.reshape(-1, block, block)
-    near_product = fetch_halo(
+    (near_product,) = fetch_halo(
         flat_product, lambda core: 0, flat_product, CHUNKS, share // CHUNKS, 1
     )
     moves = [(0, slice(None), 0, share), (1, 8, share, share)]
@@ -405,16 +496,17 @@
         for h in range(2):
             moves.append((1, j + 4 * h, (2 * j + 2 + h) * share, share))
     metric = block_products(
-        table,
-        groups,
+        tiles,
+        (metric_entries, metric_pairs),
         [flat_product, near_product, flat_factor, near.reshape(-1, block, block)],
         moves,
         [],
         rows,
         slots,
         5 * rows * kept,
-        entry_at,
+        True,
         half_x,
+        n,
     )
     return (product, metric)
 

time: 312 us -> 300 us (0.962); the launches traced: 312 us -> 296 us
  other arithmetic: 14.6 us -> 0 us
  starting transfers between devices: 9.02 us -> 0 us
  Pallas kernels: 285 us -> 293 us
    pallas_call x2, Pallas kernels: 77.5 us -> 89.1 us  [block_products(): pl.pallas_call(kernel, out_shape=jax.ShapeDtypeStruct((rows * outs, block...]
    reduce_sum x12 -> x0, other arithmetic: 11.5 us -> none  [the longest x2 2.87 us: packed_list(): count = jnp.sum(found, axis=-1)]
    ppermute x5 -> x0, starting transfers between devices: 9.02 us -> none  [the longest x4 7.5 us: shards(): lax.ppermute(patterns, 'rows', [(s, (s - o) % n) for s in range(n)])]
    pallas_call x2, Pallas kernels: 208 us -> 204 us  [fetch_halo(): pl.pallas_call(kernel, out_shape=out_shape, in_specs=[anywhere] * len(ope...]
  transfers between devices with their start and end apart: 5 -> 0, of which waited for: 1 -> 0; matrix products, arithmetic and copies ran while one was open for 1% -> 0% of each run, Pallas kernels for 0% -> 0%
where the time goes in v3:
time: 300 us; the launch traced here: 296 us
  Pallas kernels  293 us (98%)
    pallas_call x2, Pallas kernels, fetch_halo(): pl.pallas_call(kernel, out_shape=out_shape, in_specs=[anywhere] * len(ope...  204 us
    pallas_call x2, Pallas kernels, block_products(): pl.pallas_call(kernel, out_shape=jax.ShapeDtypeStruct((rows * outs, block...  89.1 us

profile of v3, /device:TPU:1, one launch (start us, length us, event | category | flops | bytes accessed | tf_op | source)
XLA Modules:
  0.0 295.8 jit_solution(6209629215712444123)
XLA Ops:
  0.7 0.8 concatenate.3
  1.5 0.6 pad.4.refs_2_
  2.1 85.2 %shard_map.77 = (f32[10,32,128,128]{3,2,1,0:T(8,128)}, s32[6,8,128]{2,1,0:T(8,128)}) custom-call(f32[64,128,128]{2,1,0:T(8,128)} %bitcast.6, f32[32,128,128]{2,1,0:T(8,128)} %bitcast.9, s32[8,128]{1,0:T(8,128)} %pad.4.refs_2_), custom_call_target="tpu_custom_call" | custom-call | tf_op jit(solution)/shard_map/pallas_call | solution.py:205
  87.3 0.0 copy-start
  87.3 0.7 copy-done
  88.1 37.3 %shard_map.78.refs_0_.refs_1_ = f32[48,128,128]{2,1,0:T(8,128)} custom-call(s32[6,8,128]{2,1,0:T(8,128)S(1)} %copy-done, f32[64,128,128]{2,1,0:T(8,128)} %bitcast.7, f32[10,32,128,128]{3,2,1,0:T(8,128)} %get-tuple-element.5.refs_2_, f32[32,128,128]{2,1,0:T(8,128)} %bitcast.10), custom_call_target="tpu_custom_call" | custom-call | flops 24159191040 | bytes 28311552 | tf_op jit(solution)/shard_map/pallas_call | solution.py:338
  125.3 0.0 copy-start.1
  125.4 118.6 %shard_map.79.refs_2_ = f32[10,48,128,128]{3,2,1,0:T(8,128)} custom-call(f32[48,128,128]{2,1,0:T(8,128)} %shard_map.78.refs_0_.refs_1_, f32[48,128,128]{2,1,0:T(8,128)} %shard_map.78.refs_0_.refs_1_), custom_call_target="tpu_custom_call" | custom-call | tf_op jit(solution)/shard_map/pallas_call | solution.py:205
  243.9 0.0 copy-done.1
  244.0 51.8 %shard_map.80 = f32[48,128,128]{2,1,0:T(8,128)} custom-call(s32[6,8,128]{2,1,0:T(8,128)S(1)} %copy-done.1, f32[48,128,128]{2,1,0:T(8,128)} %shard_map.78.refs_0_.refs_1_, f32[10,48,128,128]{3,2,1,0:T(8,128)} %shard_map.79.refs_2_, f32[64,128,128]{2,1,0:T(8,128)} %bitcast.8, f32[320,128,128]{2,1,0:T(8,128)} %bitcast.11), custom_call_target="tpu_custom_call" | custom-call | flops 24159191040 | bytes 38797312 | tf_op jit(solution)/shard_map/pallas_call | solution.py:338
  (2 shorter events, 0.0 us)
Async XLA Ops:
  87.3 0.7 copy-start
  125.3 118.6 %copy-start.1 = (s32[6,8,128]{2,1,0:T(8,128)S(1)}, s32[6,8,128]{2,1,0:T(8,128)}, u32[]{:S(2)}) copy-start(s32[6,8,128]{2,1,0:T(8,128)} %get-tuple-element.4.refs_0_) | copy-start | bytes 73732

commit v4 on v3

--- a/solution.py
+++ b/solution.py
@@ -8,7 +8,7 @@
 MESH = pl.DeviceIdType.MESH
 CHUNKS = 8
 GROUP = 4
-TOGETHER = 2
+TOGETHER = 4
 CODE = 1024
 
 
@@ -232,9 +232,24 @@
         copies = [moved(i, move, pool, sems) for i, move in enumerate(moves)]
         for copy in lhs_copies + copies:
             copy.start()
-        build_entries, build_pairs = build
+        total = n * rows
+
+        def clear(i, carry):
+            for e in range(slots):
+                table_ref[i * slots + e] = jnp.int32(pool_blocks)
+            return carry
+
+        lax.fori_loop(0, rows * outs, clear, 0)
+
+        def forget(i, carry):
+            for e in range(16):
+                where_ref[i * 16 + e] = jnp.int32(pool_blocks)
+            return carry
+
+        lax.fori_loop(0, 5 * rows * total // 16, forget, 0)
+        place_rows, entries, base_of, column_of = build
         if transposed:
-            build_entries(tiles_ref, entry_ref, count_ref)
+            entries(tiles_ref, where_ref, entry_ref, pool_blocks)
             first, second = source_refs[-2:]
             bound = first.shape[0]
 
@@ -256,27 +271,25 @@
             lax.fori_loop(0, rows * slots, fetch, 0)
         pool[pool_blocks] = jnp.zeros((block, block), jnp.float32)
 
-        def clear(i, carry):
-            for e in range(slots):
-                table_ref[i * slots + e] = jnp.int32(pool_blocks)
-            return carry
-
-        lax.fori_loop(0, rows * outs, clear, 0)
-
-        def forget(i, carry):
-            for e in range(rows):
-                where_ref[i * rows + e] = jnp.int32(outs)
-            return carry
-
-        lax.fori_loop(0, n, forget, 0)
-        lax.fori_loop(
-            0,
-            rows,
-            lambda row, carry: build_pairs(
-                row, tiles_ref, table_ref, count_ref, where_ref, entry_ref
-            ),
-            0,
-        )
+        place_rows(tiles_ref, where_ref)
+
+        def list_row(row, carry):
+            bases = [base_of(tiles_ref, entry_ref, row, e) * total for e in range(slots)]
+
+            def list_output(o, carry):
+                column = column_of(tiles_ref, row, o)
+                start = (row * outs + o) * slots
+                count = jnp.int32(0)
+                for e in range(slots):
+                    at = where_ref[bases[e] + column]
+                    table_ref[start + count] = at + e * CODE
+                    count = count + jnp.where(at != pool_blocks, 1, 0)
+                count_ref[row * outs + o] = count
+                return carry
+
+            return lax.fori_loop(0, outs, list_output, carry)
+
+        lax.fori_loop(0, rows, list_row, 0)
         for copy in lhs_copies:
             copy.wait()
 
@@ -314,10 +327,9 @@
 
         def some_outputs(index, carry):
             first = index * TOGETHER
-            counts = first // outs * (outs + 1) + first % outs
-            steps = count_ref[counts]
+            steps = count_ref[first]
             for e in range(1, TOGETHER):
-                steps = jnp.maximum(steps, count_ref[counts + e])
+                steps = jnp.maximum(steps, count_ref[first + e])
             steps = (steps + GROUP - 1) // GROUP
 
             def one_group(g, totals):
@@ -347,10 +359,10 @@
             pltpu.VMEM((rows * slots, block, block), jnp.bfloat16),
             pltpu.SemaphoreType.DMA((len(moves),)),
             pltpu.SemaphoreType.DMA((rows * slots,)),
-            pltpu.SMEM((rows * outs * slots + 2048,), jnp.int32),
-            pltpu.SMEM((rows * (outs + 1) + 8,), jnp.int32),
-            pltpu.SMEM((n * rows,), jnp.int32),
-            pltpu.SMEM((rows * 2 * slots + 1024,), jnp.int32),
+            pltpu.SMEM((rows * outs * slots,), jnp.int32),
+            pltpu.SMEM((rows * outs,), jnp.int32),
+            pltpu.SMEM((5 * rows * n * rows,), jnp.int32),
+            pltpu.SMEM((rows * 2 * slots,), jnp.int32),
         ],
         compiler_params=pltpu.CompilerParams(vmem_limit_bytes=52 * 1024 * 1024),
         cost_estimate=pl.CostEstimate(
@@ -369,6 +381,7 @@
     n = lax.axis_size("rows")
     r = lax.axis_index("rows")
     q = lax.axis_index("rep")
+    total = n * rows
     mine = margin_blocks.shape[1]
     at_kept, at_margin = slots, slots + kept
     at_metric = at_margin + mine
@@ -382,81 +395,79 @@
     def place_of(tiles):
         return tiles[0, 0, at_place], tiles[0, 0, at_place + 1]
 
-    def append(row, out, code, outs, table, counts):
-        count = counts[row * (outs + 1) + out]
-        start = jnp.where(out == outs, rows * outs, row * outs + out)
-        table[start * slots + count] = code
-        counts[row * (outs + 1) + out] = count + 1
-
-    def product_pairs(row, tiles, table, counts, where, entry):
-        mr, mq = place_of(tiles)
+    def place_factor(tiles, where):
+        _, mq = place_of(tiles)
+
+        def one_row(near_row, carry):
+            slot, inner = near_row // rows, near_row % rows
+            swapped = ((inner // half_rows) ^ mq) * half_rows + inner % half_rows
+            base = (slot * rows + jnp.where(slot == 0, inner, swapped)) * slots
+            for m in range(slots):
+                where[near_row * total + tiles[slot, inner, m]] = base + m
+            return carry
+
+        lax.fori_loop(0, 5 * rows, one_row, 0)
+
+    def margin_row(tiles, entry, row, k):
+        mr, _ = place_of(tiles)
         sign_x = 1 - 2 * (mr % 2)
         sign_y = 2 - 4 * (mr // 2 % 2)
-        for y in range(half_kept):
-            where[tiles[0, row, at_kept + mq * half_kept + y]] = jnp.int32(y)
-        for y in range(half_kept + 1):
-            counts[row * (half_kept + 1) + y] = jnp.int32(0)
-
-        def one_margin(k, carry):
-            theirs = k // mine
-            column = tiles[5 * theirs, row, at_margin + k % mine]
-            offset = (column // rows - mr + 2 + n) % n - 2
-            slot = jnp.where(offset == sign_x, 1, jnp.where(offset == sign_y, 2, 3))
-            slot = jnp.where(offset == -sign_x, 4, jnp.where(offset == 0, 0, slot))
-            inner = column % rows
-            swapped = ((inner // half_rows) ^ mq) * half_rows + inner % half_rows
-            base = k * CODE + (slot * rows + jnp.where(slot == 0, inner, swapped)) * slots
-            for m in range(slots):
-                out = where[tiles[slot, inner, m]]
-                append(row, out, base + m, half_kept, table, counts)
-            return carry
-
-        lax.fori_loop(0, 2 * mine, one_margin, 0)
-        for y in range(half_kept):
-            where[tiles[0, row, at_kept + mq * half_kept + y]] = jnp.int32(half_kept)
-        return 0
-
-    def metric_entries(tiles, entry, counts):
+        column = tiles[5 * (k // mine), row, at_margin + k % mine]
+        offset = (column // rows - mr + 2 + n) % n - 2
+        slot = jnp.where(offset == sign_x, 1, jnp.where(offset == sign_y, 2, 3))
+        slot = jnp.where(offset == -sign_x, 4, jnp.where(offset == 0, 0, slot))
+        return slot * rows + column % rows
+
+    def product_column(tiles, row, y):
+        return tiles[0, row, at_kept + place_of(tiles)[1] * half_kept + y]
+
+    def metric_entries(tiles, where, entry, missing):
         mr, mq = place_of(tiles)
-        for a in range(rows + 1):
-            counts[a] = jnp.int32(0)
+
+        def each_block(visit):
+            def one_row(near_row, carry):
+                slot, inner = near_row // rows, near_row % rows
+                other = (inner // half_rows) ^ mq
+                held = rows + (slot - 1 + 4 * other) * half_rows + inner % half_rows
+                base = jnp.where(slot == 0, inner, held) * slots
+                for m in range(slots):
+                    where[near_row * total + tiles[slot, inner, m]] = visit(base + m)
+                return carry
+
+            lax.fori_loop(0, 5 * rows, one_row, 0)
+
+        each_block(lambda at: at + missing + 1)
+
+        def one_column(a, carry):
+            count = jnp.int32(0)
+            for near_row in range(5 * rows):
+                at = where[near_row * total + mr * rows + a]
+                entry[a * 2 * slots + count] = (at - missing - 1) * CODE + near_row
+                count = count + jnp.where(at != missing, 1, 0)
+            return carry
+
+        lax.fori_loop(0, rows, one_column, 0)
+        each_block(lambda at: jnp.int32(missing))
+
+    def place_product(tiles, where):
+        _, mq = place_of(tiles)
 
         def one_row(near_row, carry):
             slot, inner = near_row // rows, near_row % rows
-            other = (inner // half_rows) ^ mq
-            held = rows + (slot - 1 + 4 * other) * half_rows + inner % half_rows
-            base = jnp.where(slot == 0, inner, held) * slots
-            for m in range(slots):
-                a = tiles[slot, inner, m] - mr * rows
-                a = jnp.where((a >= 0) & (a < rows), a, rows)
-                count = counts[a]
-                entry[a * 2 * slots + count] = (base + m) * CODE + near_row
-                counts[a] = count + 1
+            for h in range(2):
+                base = ((2 * slot + (h ^ mq)) * rows + inner) * half_kept
+                for y in range(half_kept):
+                    column = tiles[slot, inner, at_kept + h * half_kept + y]
+                    where[near_row * total + column] = base + y
             return carry
 
         lax.fori_loop(0, 5 * rows, one_row, 0)
 
-    def metric_pairs(row, tiles, table, counts, where, entry):
-        mr, mq = place_of(tiles)
-        for x in range(half_x):
-            where[tiles[0, row, at_metric + mq * half_x + x]] = jnp.int32(x)
-        for x in range(half_x + 1):
-            counts[row * (half_x + 1) + x] = jnp.int32(0)
-
-        def one_entry(t, carry):
-            near_row = entry[row * 2 * slots + t] % CODE
-            slot, inner = near_row // rows, near_row % rows
-            for h in range(2):
-                base = ((2 * slot + (h ^ mq)) * rows + inner) * half_kept + t * CODE
-                for y in range(half_kept):
-                    out = where[tiles[slot, inner, at_kept + h * half_kept + y]]
-                    append(row, out, base + y, half_x, table, counts)
-            return carry
-
-        lax.fori_loop(0, slots, one_entry, 0)
-        for x in range(half_x):
-            where[tiles[0, row, at_metric + mq * half_x + x]] = jnp.int32(half_x)
-        return 0
+    def entry_row(tiles, entry, row, t):
+        return entry[row * 2 * slots + t] % CODE
+
+    def metric_column(tiles, row, x):
+        return tiles[0, row, at_metric + place_of(tiles)[1] * half_x + x]
 
     share = half_rows * slots
     flat_factor = factor_blocks.reshape(-1, block, block)
@@ -474,7 +485,7 @@
         lhs_moves.append((1, (8, pl.ds(row * mine, mine)), row * slots + mine, mine))
     product = block_products(
         tiles,
-        (None, product_pairs),
+        (place_factor, None, margin_row, product_column),
         [flat_factor, near, flat_margin],
         moves,
         lhs_moves,
@@ -497,7 +508,7 @@
             moves.append((1, j + 4 * h, (2 * j + 2 + h) * share, share))
     metric = block_products(
         tiles,
-        (metric_entries, metric_pairs),
+        (place_product, metric_entries, entry_row, metric_column),
         [flat_product, near_product, flat_factor, near.reshape(-1, block, block)],
         moves,
         [],

time: 300 us -> 288 us (0.960); the launches traced: 296 us -> 288 us
  Pallas kernels: 293 us -> 285 us
    pallas_call x2, Pallas kernels: 89.1 us -> 80.2 us  [block_products(): pl.pallas_call(kernel, out_shape=jax.ShapeDtypeStruct((rows * outs, block...]
where the time goes in v4:
time: 288 us
  Pallas kernels  285 us (99%)
    pallas_call x2, Pallas kernels, fetch_halo(): pl.pallas_call(kernel, out_shape=out_shape, in_specs=[anywhere] * len(ope...  205 us
    pallas_call x2, Pallas kernels, block_products(): pl.pallas_call(kernel, out_shape=jax.ShapeDtypeStruct((rows * outs, block...  80.2 us

profile of v4, /device:TPU:1, one launch (start us, length us, event | category | flops | bytes accessed | tf_op | source)
XLA Modules:
  0.0 287.7 jit_solution(8961079965262759203)
XLA Ops:
  0.7 0.8 concatenate.3
  1.5 0.6 pad.4.refs_2_
  2.1 85.2 %shard_map.77 = (f32[10,32,128,128]{3,2,1,0:T(8,128)}, s32[6,8,128]{2,1,0:T(8,128)}) custom-call(f32[64,128,128]{2,1,0:T(8,128)} %bitcast.6, f32[32,128,128]{2,1,0:T(8,128)} %bitcast.9, s32[8,128]{1,0:T(8,128)} %pad.4.refs_2_), custom_call_target="tpu_custom_call" | custom-call | tf_op jit(solution)/shard_map/pallas_call | solution.py:205
  87.3 0.0 copy-start
  87.3 0.7 copy-done
  88.1 34.1 %shard_map.78.refs_0_.refs_1_ = f32[48,128,128]{2,1,0:T(8,128)} custom-call(s32[6,8,128]{2,1,0:T(8,128)S(1)} %copy-done, f32[64,128,128]{2,1,0:T(8,128)} %bitcast.7, f32[10,32,128,128]{3,2,1,0:T(8,128)} %get-tuple-element.5.refs_2_, f32[32,128,128]{2,1,0:T(8,128)} %bitcast.10), custom_call_target="tpu_custom_call" | custom-call | flops 24159191040 | bytes 28311552 | tf_op jit(solution)/shard_map/pallas_call | solution.py:350
  122.1 0.0 copy-start.1
  122.2 119.4 %shard_map.79.refs_2_ = f32[10,48,128,128]{3,2,1,0:T(8,128)} custom-call(f32[48,128,128]{2,1,0:T(8,128)} %shard_map.78.refs_0_.refs_1_, f32[48,128,128]{2,1,0:T(8,128)} %shard_map.78.refs_0_.refs_1_), custom_call_target="tpu_custom_call" | custom-call | tf_op jit(solution)/shard_map/pallas_call | solution.py:205
  241.6 0.0 copy-done.1
  241.6 46.1 %shard_map.80 = f32[48,128,128]{2,1,0:T(8,128)} custom-call(s32[6,8,128]{2,1,0:T(8,128)S(1)} %copy-done.1, f32[48,128,128]{2,1,0:T(8,128)} %shard_map.78.refs_0_.refs_1_, f32[10,48,128,128]{3,2,1,0:T(8,128)} %shard_map.79.refs_2_, f32[64,128,128]{2,1,0:T(8,128)} %bitcast.8, f32[320,128,128]{2,1,0:T(8,128)} %bitcast.11), custom_call_target="tpu_custom_call" | custom-call | flops 24159191040 | bytes 38797312 | tf_op jit(solution)/shard_map/pallas_call | solution.py:350
  (2 shorter events, 0.0 us)
Async XLA Ops:
  87.3 0.7 copy-start
  122.1 119.4 %copy-start.1 = (s32[6,8,128]{2,1,0:T(8,128)S(1)}, s32[6,8,128]{2,1,0:T(8,128)}, u32[]{:S(2)}) copy-start(s32[6,8,128]{2,1,0:T(8,128)} %get-tuple-element.4.refs_0_) | copy-start | bytes 73732

commit v5 on v4

--- a/solution.py
+++ b/solution.py
@@ -6,7 +6,7 @@
 from jax.sharding import PartitionSpec as P
 
 MESH = pl.DeviceIdType.MESH
-CHUNKS = 8
+CHUNKS = 16
 GROUP = 4
 TOGETHER = 4
 CODE = 1024
@@ -105,7 +105,7 @@
         pairs = [(c, c + 1) for c in range(0, chunks, 2)]
         x_order = [b for a, b in pairs] + [a for a, b in pairs]
         y_order = [a for a, b in pairs] + [b for a, b in pairs]
-        ahead = 2
+        ahead = chunks // 4
         for i in range(ahead):
             over_x(x_order[i]).start()
             over_y(y_order[i]).start()
@@ -317,13 +317,15 @@
                 value = pool[code % CODE]
                 top = value.astype(jnp.bfloat16)
                 rest = (value - top.astype(jnp.float32)).astype(jnp.bfloat16)
-                left += [high[s], high[s], low[s]]
-                right += [top, rest, top]
-            return jnp.dot(
+                left.append(jnp.concatenate([high[s], low[s]], axis=0))
+                right.append(jnp.concatenate([top, rest], axis=1))
+            both = jnp.dot(
                 jnp.concatenate(left, axis=1),
                 jnp.concatenate(right, axis=0),
                 preferred_element_type=jnp.float32,
             )
+            upper = both[:block, :block] + both[:block, block:]
+            return upper + (both[block:, :block] + both[block:, block:])
 
         def some_outputs(index, carry):
             first = index * TOGETHER

time: 288 us -> 290 us (level)
    pallas_call x2, Pallas kernels: 205 us -> 213 us  [fetch_halo(): pl.pallas_call(kernel, out_shape=out_shape, in_specs=[anywhere] * len(ope...]
    pallas_call x2, Pallas kernels: 80.2 us -> 72.6 us  [block_products(): pl.pallas_call(kernel, out_shape=jax.ShapeDtypeStruct((rows * outs, block...]
where the time goes in v5:
time: 290 us; the launch traced here: 288 us
  Pallas kernels  285 us (98%)
    pallas_call x2, Pallas kernels, fetch_halo(): pl.pallas_call(kernel, out_shape=out_shape, in_specs=[anywhere] * len(ope...  213 us
    pallas_call x2, Pallas kernels, block_products(): pl.pallas_call(kernel, out_shape=jax.ShapeDtypeStruct((rows * outs, block...  72.6 us

profile of v5, /device:TPU:1, one launch (start us, length us, event | category | flops | bytes accessed | tf_op | source)
XLA Modules:
  0.0 288.3 jit_solution(7408548050166738612)
XLA Ops:
  0.7 0.8 concatenate.3
  1.5 0.6 pad.4.refs_2_
  2.1 90.3 %shard_map.77 = (f32[10,32,128,128]{3,2,1,0:T(8,128)}, s32[6,8,128]{2,1,0:T(8,128)}) custom-call(f32[64,128,128]{2,1,0:T(8,128)} %bitcast.6, f32[32,128,128]{2,1,0:T(8,128)} %bitcast.9, s32[8,128]{1,0:T(8,128)} %pad.4.refs_2_), custom_call_target="tpu_custom_call" | custom-call | tf_op jit(solution)/shard_map/pallas_call | solution.py:205
  92.4 0.0 copy-start
  92.4 0.7 copy-done
  93.1 31.5 %shard_map.78.refs_0_.refs_1_ = f32[48,128,128]{2,1,0:T(8,128)} custom-call(s32[6,8,128]{2,1,0:T(8,128)S(1)} %copy-done, f32[64,128,128]{2,1,0:T(8,128)} %bitcast.7, f32[10,32,128,128]{3,2,1,0:T(8,128)} %get-tuple-element.5.refs_2_, f32[32,128,128]{2,1,0:T(8,128)} %bitcast.10), custom_call_target="tpu_custom_call" | custom-call | flops 24159191040 | bytes 28311552 | tf_op jit(solution)/shard_map/pallas_call | solution.py:352
  124.7 0.0 copy-start.1
  124.7 122.5 %shard_map.79.refs_2_ = f32[10,48,128,128]{3,2,1,0:T(8,128)} custom-call(f32[48,128,128]{2,1,0:T(8,128)} %shard_map.78.refs_0_.refs_1_, f32[48,128,128]{2,1,0:T(8,128)} %shard_map.78.refs_0_.refs_1_), custom_call_target="tpu_custom_call" | custom-call | tf_op jit(solution)/shard_map/pallas_call | solution.py:205
  247.2 0.0 copy-done.1
  247.2 41.1 %shard_map.80 = f32[48,128,128]{2,1,0:T(8,128)} custom-call(s32[6,8,128]{2,1,0:T(8,128)S(1)} %copy-done.1, f32[48,128,128]{2,1,0:T(8,128)} %shard_map.78.refs_0_.refs_1_, f32[10,48,128,128]{3,2,1,0:T(8,128)} %shard_map.79.refs_2_, f32[64,128,128]{2,1,0:T(8,128)} %bitcast.8, f32[320,128,128]{2,1,0:T(8,128)} %bitcast.11), custom_call_target="tpu_custom_call" | custom-call | flops 24159191040 | bytes 38797312 | tf_op jit(solution)/shard_map/pallas_call | solution.py:352
  (2 shorter events, 0.0 us)
Async XLA Ops:
  92.4 0.7 copy-start
  124.7 122.5 %copy-start.1 = (s32[6,8,128]{2,1,0:T(8,128)S(1)}, s32[6,8,128]{2,1,0:T(8,128)}, u32[]{:S(2)}) copy-start(s32[6,8,128]{2,1,0:T(8,128)} %get-tuple-element.4.refs_0_) | copy-start | bytes 73732

commit v6 on v5

--- a/solution.py
+++ b/solution.py
@@ -6,9 +6,9 @@
 from jax.sharding import PartitionSpec as P
 
 MESH = pl.DeviceIdType.MESH
-CHUNKS = 16
-GROUP = 4
-TOGETHER = 4
+CHUNKS = 8
+GROUP = 2
+TOGETHER = 6
 CODE = 1024
 
 
@@ -73,8 +73,14 @@
         def share(place, c):
             return copy(out_ref.at[place, span(c)], 4 + place, 4 + place, c, (r, 1 - q))
 
-        def own_share(c):
-            return copy(swapped_ref.at[span(c)], 8, at_swap, c, (r, 1 - q))
+        own_share = pltpu.make_async_remote_copy(
+            src_ref=swapped_ref,
+            dst_ref=out_ref.at[at_swap],
+            send_sem=send_sem.at[8, 0],
+            recv_sem=recv_sem.at[at_swap, 0],
+            device_id=(r, 1 - q),
+            device_id_type=MESH,
+        )
 
         def arrived(place, c):
             copy(out_ref.at[place, span(c)], 0, place, c, (r, 1 - q)).wait_recv()
@@ -120,7 +126,8 @@
             if i + ahead < chunks:
                 over_x(x_order[i + ahead]).start()
             share(at_x, c).start()
-            own_share(i).start()
+            if i == 0:
+                own_share.start()
             c = y_order[i]
             arrived(at_y, c)
             over_z(c).start()
@@ -177,7 +184,7 @@
         arrived(at_z, c)
         share(at_z, c).start()
         for c in range(chunks):
-            for place in (4, 5, 6, 7, at_swap):
+            for place in (4, 5, 6, 7):
                 arrived(place, c)
         for c in range(chunks):
             over_x(c).wait_send()
@@ -192,7 +199,7 @@
 
             for place in (at_x, at_y, at_z, at_second):
                 share(place, c).wait_send()
-            own_share(c).wait_send()
+        own_share.wait()
 
     anywhere = pl.BlockSpec(memory_space=pl.ANY)
     out_shape = [jax.ShapeDtypeStruct((10, chunks * size, block, block), jnp.float32)]

time: 290 us -> 286 us (0.986)
  Pallas kernels: 285 us -> 281 us
    pallas_call x2, Pallas kernels: 213 us -> 206 us  [fetch_halo(): pl.pallas_call(kernel, out_shape=out_shape, in_specs=[anywhere] * len(ope...]
where the time goes in v6:
time: 286 us; the launch traced here: 284 us
  Pallas kernels  281 us (98%)
    pallas_call x2, Pallas kernels, fetch_halo(): pl.pallas_call(kernel, out_shape=out_shape, in_specs=[anywhere] * len(ope...  206 us
    pallas_call x2, Pallas kernels, block_products(): pl.pallas_call(kernel, out_shape=jax.ShapeDtypeStruct((rows * outs, block...  74.6 us

profile of v6, /device:TPU:1, one launch (start us, length us, event | category | flops | bytes accessed | tf_op | source)
XLA Modules:
  0.0 283.6 jit_solution(11930327587576370108)
XLA Ops:
  0.7 0.8 concatenate.3
  1.5 0.6 pad.4.refs_2_
  2.1 85.2 %shard_map.77 = (f32[10,32,128,128]{3,2,1,0:T(8,128)}, s32[6,8,128]{2,1,0:T(8,128)}) custom-call(f32[64,128,128]{2,1,0:T(8,128)} %bitcast.6, f32[32,128,128]{2,1,0:T(8,128)} %bitcast.9, s32[8,128]{1,0:T(8,128)} %pad.4.refs_2_), custom_call_target="tpu_custom_call" | custom-call | tf_op jit(solution)/shard_map/pallas_call | solution.py:212
  87.3 0.0 copy-start
  87.3 0.7 copy-done
  88.1 32.4 %shard_map.78.refs_0_.refs_1_ = f32[48,128,128]{2,1,0:T(8,128)} custom-call(s32[6,8,128]{2,1,0:T(8,128)S(1)} %copy-done, f32[64,128,128]{2,1,0:T(8,128)} %bitcast.7, f32[10,32,128,128]{3,2,1,0:T(8,128)} %get-tuple-element.5.refs_2_, f32[32,128,128]{2,1,0:T(8,128)} %bitcast.10), custom_call_target="tpu_custom_call" | custom-call | flops 24159191040 | bytes 28311552 | tf_op jit(solution)/shard_map/pallas_call | solution.py:359
  120.5 0.0 copy-start.1
  120.5 120.9 %shard_map.79.refs_2_ = f32[10,48,128,128]{3,2,1,0:T(8,128)} custom-call(f32[48,128,128]{2,1,0:T(8,128)} %shard_map.78.refs_0_.refs_1_, f32[48,128,128]{2,1,0:T(8,128)} %shard_map.78.refs_0_.refs_1_), custom_call_target="tpu_custom_call" | custom-call | tf_op jit(solution)/shard_map/pallas_call | solution.py:212
  241.4 0.0 copy-done.1
  241.4 42.2 %shard_map.80 = f32[48,128,128]{2,1,0:T(8,128)} custom-call(s32[6,8,128]{2,1,0:T(8,128)S(1)} %copy-done.1, f32[48,128,128]{2,1,0:T(8,128)} %shard_map.78.refs_0_.refs_1_, f32[10,48,128,128]{3,2,1,0:T(8,128)} %shard_map.79.refs_2_, f32[64,128,128]{2,1,0:T(8,128)} %bitcast.8, f32[320,128,128]{2,1,0:T(8,128)} %bitcast.11), custom_call_target="tpu_custom_call" | custom-call | flops 24159191040 | bytes 38797312 | tf_op jit(solution)/shard_map/pallas_call | solution.py:359
  (2 shorter events, 0.0 us)
Async XLA Ops:
  87.3 0.7 copy-start
  120.5 120.9 %copy-start.1 = (s32[6,8,128]{2,1,0:T(8,128)S(1)}, s32[6,8,128]{2,1,0:T(8,128)}, u32[]{:S(2)}) copy-start(s32[6,8,128]{2,1,0:T(8,128)} %get-tuple-element.4.refs_0_) | copy-start | bytes 73732

commit v7 on v6

--- a/solution.py
+++ b/solution.py
@@ -7,8 +7,8 @@
 
 MESH = pl.DeviceIdType.MESH
 CHUNKS = 8
-GROUP = 2
-TOGETHER = 6
+GROUP = 4
+TOGETHER = 4
 CODE = 1024
 
 
@@ -237,7 +237,8 @@
 
         lhs_copies = [moved(i, move, lhs, lhs_sems) for i, move in enumerate(lhs_moves)]
         copies = [moved(i, move, pool, sems) for i, move in enumerate(moves)]
-        for copy in lhs_copies + copies:
+        early = len(copies) // 3 if transposed else len(copies)
+        for copy in lhs_copies + copies[:early]:
             copy.start()
         total = n * rows
 
@@ -276,6 +277,8 @@
                 return carry
 
             lax.fori_loop(0, rows * slots, fetch, 0)
+        for copy in copies[early:]:
+            copy.start()
         pool[pool_blocks] = jnp.zeros((block, block), jnp.float32)
 
         place_rows(tiles_ref, where_ref)

time: 286 us -> 279 us (0.976)
  Pallas kernels: 281 us -> 275 us
    pallas_call x2, Pallas kernels: 74.6 us -> 69 us  [block_products(): pl.pallas_call(kernel, out_shape=jax.ShapeDtypeStruct((rows * outs, block...]
where the time goes in v7:
time: 279 us; the launch traced here: 278 us
  Pallas kernels  275 us (99%)
    pallas_call x2, Pallas kernels, fetch_halo(): pl.pallas_call(kernel, out_shape=out_shape, in_specs=[anywhere] * len(ope...  206 us
    pallas_call x2, Pallas kernels, block_products(): pl.pallas_call(kernel, out_shape=jax.ShapeDtypeStruct((rows * outs, block...  69 us

profile of v7, /device:TPU:1, one launch (start us, length us, event | category | flops | bytes accessed | tf_op | source)
XLA Modules:
  0.0 277.6 jit_solution(8568344623352309429)
XLA Ops:
  0.7 0.8 concatenate.3
  1.5 0.6 pad.4.refs_2_
  2.1 85.2 %shard_map.77 = (f32[10,32,128,128]{3,2,1,0:T(8,128)}, s32[6,8,128]{2,1,0:T(8,128)}) custom-call(f32[64,128,128]{2,1,0:T(8,128)} %bitcast.6, f32[32,128,128]{2,1,0:T(8,128)} %bitcast.9, s32[8,128]{1,0:T(8,128)} %pad.4.refs_2_), custom_call_target="tpu_custom_call" | custom-call | tf_op jit(solution)/shard_map/pallas_call | solution.py:212
  87.3 0.0 copy-start
  87.3 0.7 copy-done
  88.1 29.7 %shard_map.78.refs_0_.refs_1_ = f32[48,128,128]{2,1,0:T(8,128)} custom-call(s32[6,8,128]{2,1,0:T(8,128)S(1)} %copy-done, f32[64,128,128]{2,1,0:T(8,128)} %bitcast.7, f32[10,32,128,128]{3,2,1,0:T(8,128)} %get-tuple-element.5.refs_2_, f32[32,128,128]{2,1,0:T(8,128)} %bitcast.10), custom_call_target="tpu_custom_call" | custom-call | flops 24159191040 | bytes 28311552 | tf_op jit(solution)/shard_map/pallas_call | solution.py:362
  117.7 0.0 copy-start.1
  117.7 120.5 %shard_map.79.refs_2_ = f32[10,48,128,128]{3,2,1,0:T(8,128)} custom-call(f32[48,128,128]{2,1,0:T(8,128)} %shard_map.78.refs_0_.refs_1_, f32[48,128,128]{2,1,0:T(8,128)} %shard_map.78.refs_0_.refs_1_), custom_call_target="tpu_custom_call" | custom-call | tf_op jit(solution)/shard_map/pallas_call | solution.py:212
  238.2 0.0 copy-done.1
  238.2 39.4 %shard_map.80 = f32[48,128,128]{2,1,0:T(8,128)} custom-call(s32[6,8,128]{2,1,0:T(8,128)S(1)} %copy-done.1, f32[48,128,128]{2,1,0:T(8,128)} %shard_map.78.refs_0_.refs_1_, f32[10,48,128,128]{3,2,1,0:T(8,128)} %shard_map.79.refs_2_, f32[64,128,128]{2,1,0:T(8,128)} %bitcast.8, f32[320,128,128]{2,1,0:T(8,128)} %bitcast.11), custom_call_target="tpu_custom_call" | custom-call | flops 24159191040 | bytes 38797312 | tf_op jit(solution)/shard_map/pallas_call | solution.py:362
  (2 shorter events, 0.0 us)
Async XLA Ops:
  87.3 0.7 copy-start
  117.7 120.5 %copy-start.1 = (s32[6,8,128]{2,1,0:T(8,128)S(1)}, s32[6,8,128]{2,1,0:T(8,128)}, u32[]{:S(2)}) copy-start(s32[6,8,128]{2,1,0:T(8,128)} %get-tuple-element.4.refs_0_) | copy-start | bytes 73732
